TPU v7x, 32 devices: a whole 2x2x4 slice. The times are simulated.
32 devices in a mesh: scale: 4 (over x, core), space: 8 (over z, y).
Axes of the slice: x: 2, y: 2, z: 4, core: 2. Of those that a mesh axis runs over, the one named last changes fastest.
Arguments:
- features: bfloat16 [4, 32, 128, 512], P('scale', 'space'), may hold values from -6 to 6
- valid_rows: int32 [4], replicated, may hold values from 8 to 32, as said below
- conv_master: float32 [3, 4608, 512], P(None, 'space'), may hold values from -0.125 to 0.125
- head_master: float32 [917504], P(('scale', 'space')), may hold values from -0.25 to 0.25
- vectors: float32 [5120], replicated
- conv_first: float32 [3, 4608, 512], P(None, 'space'), may hold values from -40 to 40
- conv_second: float32 [3, 4608, 512], P(None, 'space'), may hold values from 186.14845 to 744.5938
- head_first: float32 [917504], P(('scale', 'space')), may hold values from -40 to 40
- head_second: float32 [917504], P(('scale', 'space')), may hold values from 186.14845 to 744.5938
- vec_first: float32 [5120], replicated
- vec_second: float32 [5120], replicated
- statistics: float32 [3, 512, 512], replicated, as said below
- bases: float32 [3, 512, 512], replicated, as said below
- cotangent: bfloat16 [32, 128, 1792], P('space'), may hold values from -6 to 6
Outputs:
- merged: bfloat16 [32, 128, 1792], P('space')
- features_grad: bfloat16 [4, 32, 128, 512], P('scale', 'space')
- conv_first_new: float32 [3, 4608, 512], P(None, 'space')
- conv_second_new: float32 [3, 4608, 512], P(None, 'space')
- conv_new: float32 [3, 4608, 512], P(None, 'space')
- head_first_new: float32 [917504], P(('scale', 'space'))
- head_second_new: float32 [917504], P(('scale', 'space'))
- head_new: float32 [917504], P(('scale', 'space'))
- vec_first_new: float32 [5120], replicated
- vec_second_new: float32 [5120], replicated
- vec_new: float32 [5120], replicated
- statistics_new: float32 [3, 512, 512], replicated
- bases_new: float32 [3, 512, 512], replicated
Inputs may be any that keep to these rules, and one draw needn't show every extreme that they name: `valid_rows`: one scale, drawn from the seed, fills all 32 rows. `statistics`: each matrix is symmetric positive definite. `bases`: each matrix is orthogonal.
All inputs are finite; a program needn't handle non-finite values.
Results may differ from a plain program's by a relative error of at most 0.014.
Values may be sent and summed in bfloat16 or wider, within the bound.
A program may use at most 256 MiB of HBM per device.

v0:
```python
from functools import partial

import jax
import jax.experimental.pallas as pl
import jax.experimental.pallas.tpu as pltpu
import jax.numpy as jnp
from jax import lax
from jax.sharding import PartitionSpec as P

NH = 7
HD = 256
STEP = 5


BETA_ONE = 0.9
BETA_TWO = 0.95
EPSILON = 1e-08
DECAY = 0.01
RATE_CONV = 0.04
RATE_HEAD = 0.08
RATE_BIAS = 0.5
RATE_GAIN = 20.0
VMEM_LIMIT = 60 * 2**20
GELU_SCALE = 0.7978845608028654
GELU_CUBE = 0.044715


MESH = pl.DeviceIdType.MESH
LANES = 128


def place():
    scale, space = lax.axis_index("scale"), lax.axis_index("space")
    across, core = scale // 2, lax.rem(scale, 2)
    deep, side = space // 2, lax.rem(space, 2)
    return (across, core, deep, side)


def at(across, core, deep, side):
    return (2 * across + core, 2 * deep + side)


def greet(peers):
    barrier = pltpu.get_barrier_semaphore()
    for peer in peers:
        pl.semaphore_signal(barrier, inc=1, device_id=peer, device_id_type=MESH)
    pl.semaphore_wait(barrier, len(peers))


def remote(source, target, send, receive, device):
    return pltpu.make_async_remote_copy(
        src_ref=source,
        dst_ref=target,
        send_sem=send,
        recv_sem=receive,
        device_id=device,
        device_id_type=MESH,
    )


def lanes(index, count=1):
    return pl.ds(pl.multiple_of(index * LANES, LANES), count * LANES)


def partners(deep_count):
    across, core, deep, side = place()
    peers = [
        at(across, 1 - core, deep, side),
        at(1 - across, core, deep, side),
        at(across, core, deep, 1 - side),
    ]
    peers += [
        at(across, core, lax.rem(deep + hop, deep_count), side) for hop in range(1, deep_count)
    ]
    return peers


TAPS = 3


def gelu_parts(value):
    inner = GELU_SCALE * (value + GELU_CUBE * value * value * value)
    return jnp.tanh(inner)


def gelu_value(value):
    return 0.5 * value * (1.0 + gelu_parts(value))


def gelu_slope(value):
    bend = gelu_parts(value)
    rise = GELU_SCALE * (1.0 + 3.0 * GELU_CUBE * value * value)
    return 0.5 * (1.0 + bend) + 0.5 * value * (1.0 - bend * bend) * rise


def mix(left, right, left_dim, right_dim):
    return lax.dot_general(
        left,
        right,
        (((left_dim,), (right_dim,)), ((), ())),
        preferred_element_type=jnp.float32,
    )


def row_weights(valid, rows):
    scale, space = lax.axis_index("scale"), lax.axis_index("space")
    scales = lax.axis_size("scale")
    masks, weights = [], []
    for row in range(rows):
        place_in = space * rows + row
        mask = jnp.where(place_in < valid[scale], 1.0, 0.0)
        count = jnp.float32(0.0)
        for other in range(scales):
            count += jnp.where(place_in < valid[other], 1.0, 0.0)
        masks.append(mask)
        weights.append(jnp.full((1, LANES), mask) / jnp.full((1, LANES), count))
    return (masks, [weight[:, :1] for weight in weights])


def vector_lanes(vectors, start, part):
    row = start // LANES + 2 * part
    return jnp.concatenate([vectors[pl.ds(row, 1), :], vectors[pl.ds(row + 1, 1), :]], 1)


def greet_edges(peers, space_count):
    barrier = pltpu.get_barrier_semaphore()
    scale, space = lax.axis_index("scale"), lax.axis_index("space")
    for peer in peers:
        pl.semaphore_signal(barrier, inc=1, device_id=peer, device_id_type=MESH)
    next_space = space - 1 + 2 * lax.rem(space, 2)
    has_next = jnp.logical_and(next_space >= 0, next_space < space_count)

    @pl.when(has_next)
    def greet_next():
        pl.semaphore_signal(barrier, inc=1, device_id=(scale, next_space), device_id_type=MESH)

    pl.semaphore_wait(barrier, len(peers) + has_next.astype(jnp.int32))


def edge_tools(dims, halo, send_sem, receive_sem):
    rows, width, channels, space_count = dims[1], dims[2], dims[3], dims[6]
    tile = 2 * LANES
    tiles = channels // tile
    scale, space = lax.axis_index("scale"), lax.axis_index("space")
    above, below = space > 0, space < space_count - 1
    low = jnp.bfloat16

    def up(which, source):
        return remote(
            source,
            halo.at[which, 1],
            send_sem.at[which, 0],
            receive_sem.at[which, 1],
            (scale, space - 1),
        )

    def down(which, source):
        return remote(
            source,
            halo.at[which, 0],
            send_sem.at[which, 1],
            receive_sem.at[which, 0],
            (scale, space + 1),
        )

    def edge(array, row):
        return array.at[pl.ds((row + 1) * width, width), pl.ds(channels, channels)]

    def send_edges(which, array):
        @pl.when(above)
        def go_up():
            up(which, edge(array, 0)).start()

        @pl.when(below)
        def go_down():
            down(which, edge(array, rows - 1)).start()

    column = lax.broadcasted_iota(jnp.int32, (width, 1), 0)

    def put(array, slot, lane, count, value):
        here = pl.ds(slot * width, width)
        left = jnp.where(column == 0, 0.0, pltpu.roll(value, 1, 0))
        right = jnp.where(column == width - 1, 0.0, pltpu.roll(value, width - 1, 0))
        for which, moved in enumerate((left, value, right)):
            start = pl.multiple_of(which * channels + lane, LANES)
            array[here, pl.ds(start, count)] = moved.astype(low)

    def take_edges(which, array):
        for side, present, slot in ((0, above, 0), (1, below, rows + 1)):

            @pl.when(present)
            def arrived():
                if side == 0:
                    up(which, edge(array, 0)).wait_send()
                    down(which, edge(array, 0)).wait_recv()
                else:
                    down(which, edge(array, 0)).wait_send()
                    up(which, edge(array, 0)).wait_recv()
                for part in range(tiles):
                    value = halo[which, side, :, part * tile : (part + 1) * tile]
                    put(array, slot, part * tile, tile, value.astype(jnp.float32))

            @pl.when(jnp.logical_not(present))
            def missing():
                array[pl.ds(slot * width, width), :] = jnp.zeros(
                    (width, TAPS * channels), low
                )

    return (send_edges, take_edges, put)


def gather_kernel(
    dims,
    master,
    head_master,
    features,
    vectors,
    valid,
    full,
    head_full,
    wide_out,
    hidden_out,
    last_out,
    own,
    head_own,
    weights,
    wide,
    hidden,
    last,
    halo,
    local_sem,
    sends,
    receives,
    head_sends,
    head_receives,
    load_sem,
    store_sem,
    edge_sends,
    edge_receives,
):
    layers, rows, width, channels, heads, depth, space_count = dims
    deep_count = space_count // 2
    across, core, deep, side = place()
    block = 2 * core + across
    low = jnp.bfloat16
    own[0] = master[0].astype(low)
    greet_edges(partners(deep_count), space_count)

    chunks = layers * deep_count

    def split(chunk):
        rest = chunk - layers
        is_own = chunk < layers
        layer = jnp.where(is_own, chunk, rest // (deep_count - 1))
        hop = jnp.where(is_own, 0, 1 + lax.rem(rest + chunks, deep_count - 1))
        layer, hop = jnp.clip(layer, 0, layers - 1), jnp.clip(hop, 0, deep_count - 1)
        source = lax.rem(deep - hop + deep_count, deep_count)
        return (layer, hop, source, lax.rem(chunk, 2))

    def first(layer, hop):
        piece = own.at[layer, :, lanes(block)]
        target = full.at[layer, deep, side, :, lanes(block)]
        to = at(across, core, lax.rem(deep + hop, deep_count), side)
        return remote(piece, target, sends.at[0, layer, hop], receives.at[0, layer, hop], to)

    def first_in(layer, hop):
        source = lax.rem(deep - hop + deep_count, deep_count)
        piece = full.at[layer, source, side, :, lanes(block)]
        return remote(
            piece, piece, sends.at[0, layer, hop], receives.at[0, layer, hop], at(across, core, deep, side)
        )

    def second(chunk, incoming):
        layer, hop, source, odd = split(chunk)
        there_side = lax.rem(side + 1 - odd, 2)
        there_across = lax.rem(across + odd, 2)
        to = at(there_across, core, deep, there_side)
        if incoming:
            piece = full.at[layer, source, there_side, :, lanes(2 * core + there_across)]
        else:
            piece = full.at[layer, source, side, :, lanes(block)]
        return remote(piece, piece, sends.at[1, layer, hop], receives.at[1, layer, hop], to)

    def third(chunk, half, incoming):
        layer, hop, source, odd = split(chunk)
        there_side = lax.rem(side + odd, 2)
        there_across = lax.rem(across + 1 - odd, 2)
        to = at(there_across, core, deep, there_side)
        here = there_side if incoming else side
        lane = there_across if incoming else across
        piece_side = (1 - odd) * half + odd * here
        piece_lane = 2 * core + (1 - odd) * lane + odd * half
        piece = full.at[layer, source, piece_side, :, lanes(piece_lane)]
        return remote(
            piece, piece, sends.at[2 + half, layer, hop], receives.at[2 + half, layer, hop], to
        )

    def fourth(chunk, incoming):
        layer, hop, source, odd = split(chunk)
        column = 1 - core if incoming else core
        piece = full.at[layer, source, :, :, lanes(2 * column, 2)]
        to = at(across, 1 - core, deep, side)
        return remote(piece, piece, sends.at[4, layer, hop], receives.at[4, layer, hop], to)

    def local(layer):
        return pltpu.make_async_copy(
            own.at[layer, :, lanes(block)],
            full.at[layer, deep, side, :, lanes(block)],
            local_sem.at[layer],
        )

    def each(low, action):
        def step(hop, carry):
            action(hop)
            return carry

        lax.fori_loop(low, deep_count, step, 0)

    def head_local():
        return pltpu.make_async_copy(
            head_own, head_full.at[across, core, deep, side], local_sem.at[layers]
        )

    def head_first(hop):
        to = at(across, core, lax.rem(deep + hop, deep_count), side)
        target = head_full.at[across, core, deep, side]
        return remote(head_own, target, head_sends.at[hop], head_receives.at[hop], to)

    def head_first_in(hop):
        piece = head_full.at[across, core, lax.rem(deep - hop + deep_count, deep_count), side]
        to = at(across, core, deep, side)
        return remote(piece, piece, head_sends.at[hop], head_receives.at[hop], to)

    def head_next(which, incoming):
        if which == 0:
            to = at(across, core, deep, 1 - side)
            piece = head_full.at[across, core, :, 1 - side if incoming else side]
        elif which == 1:
            to = at(1 - across, core, deep, side)
            piece = head_full.at[1 - across if incoming else across, core]
        else:
            to = at(across, 1 - core, deep, side)
            piece = head_full.at[:, 1 - core if incoming else core]
        slot = deep_count + which
        return remote(piece, piece, head_sends.at[slot], head_receives.at[slot], to)

    def go_head(which):
        if which == 0:
            head_local().wait()
            each(1, lambda hop: head_first_in(hop).wait_recv())
        else:
            head_next(which - 1, True).wait_recv()
        if which < 3:
            head_next(which, False).start()

    send_edges, take_edges, put = edge_tools(dims, halo, edge_sends, edge_receives)
    tile = 2 * LANES
    tiles = channels // tile
    pixels = rows * width
    band = TAPS * channels
    masks, unused = row_weights(valid, rows)
    share = band * TAPS // space_count

    def loop(count, action):
        def body(index, carry):
            action(index)
            return carry

        lax.fori_loop(0, count, body, 0)

    def spot(index):
        return pl.multiple_of(index * tile, tile)

    def load(layer, owner):
        start = pl.multiple_of(owner * share, 8)
        return pltpu.make_async_copy(
            full.at[layer, owner // 2, lax.rem(owner, 2)],
            weights.at[layer % 2, pl.ds(start, share)],
            load_sem.at[layer % 2, owner],
        )

    def arrive(layer):
        fourth(layer, True).wait_recv()
        begin = layers + layer * (deep_count - 1)
        loop(deep_count - 1, lambda index: fourth(begin + index, True).wait_recv())
        loop(space_count, lambda owner: load(layer, owner).start())

    def store(which, layer):
        source, target = (
            (wide.at[layer], wide_out.at[layer]),
            (hidden.at[layer], hidden_out.at[layer]),
            (last, last_out),
        )[which]
        return pltpu.make_async_copy(source, target, store_sem.at[which, layer])

    def forward(layer):
        here = wide.at[layer]
        take_edges(layer, here)
        store(0, layer).start()
        loop(space_count, lambda owner: load(layer, owner).wait())

        def outer(part):
            lane = pl.ds(spot(part), tile)
            total = vector_lanes(vectors, layer * channels, part)
            for tap_row in range(TAPS):
                total += mix(
                    here[tap_row * width : tap_row * width + pixels, :],
                    weights[layer % 2, tap_row * band : (tap_row + 1) * band, lane],
                    1,
                    0,
                )
            hidden[layer, :, lane] = total
            for row in range(rows):
                span = slice(row * width, (row + 1) * width)
                value = gelu_value(hidden[layer, span, lane]) * masks[row]
                if layer < layers - 1:
                    put(wide.at[layer + 1], row + 1, spot(part), tile, value)
                else:
                    last[span, lane] = value.astype(low)

        loop(tiles, outer)
        store(1, layer).start()
        if layer < layers - 1:
            send_edges(layer + 1, wide.at[layer + 1])

    def go_second(chunk):
        layer, hop, source, odd = split(chunk)

        @pl.when(hop == 0)
        def own_rows():
            local(layer).wait()

        @pl.when(hop > 0)
        def other_rows():
            first_in(layer, hop).wait_recv()

        second(chunk, False).start()

    def go_third(chunk):
        second(chunk, True).wait_recv()
        third(chunk, 0, False).start()
        third(chunk, 1, False).start()

    def go_fourth(chunk):
        third(chunk, 0, True).wait_recv()
        third(chunk, 1, True).wait_recv()
        fourth(chunk, False).start()

    def go_head_first():
        each(1, lambda hop: head_first(hop).start())

    def go_first(layer):
        each(1, lambda hop: first(layer, hop).start())

    go_first(0)
    local(0).start()
    go_second(0)
    for layer in range(1, layers):
        own[layer] = master[layer].astype(low)
        local(layer).start()
    head_rows, head_blocks = head_own.shape[0], heads * depth // LANES
    for lane in range(head_blocks):
        head_own[:, lane * LANES : (lane + 1) * LANES] = head_master[
            pl.ds(lane, head_rows, stride=head_blocks), :
        ].astype(low)
    head_local().start()
    for row in range(rows):
        for part in range(tiles):
            value = features[row * width : (row + 1) * width, part * tile : (part + 1) * tile]
            put(wide.at[0], row + 1, part * tile, tile, value.astype(jnp.float32))
    send_edges(0, wide.at[0])

    lag_third, lag_fourth = 2, 5
    others = deep_count - 1

    def last_of(layer):
        return layers + others * (layer + 1) - 1 + lag_fourth

    early = min(2, others)
    timed = [(layers + others * (layer - 1) + early, go_first, layer) for layer in range(1, layers)]
    timed += [(layers + early, go_head_first)]
    timed += [(layers + others + 2 * which, go_head, which) for which in range(3)]
    for layer in range(layers - 1):
        timed += [(last_of(layer) + 1, arrive, layer), (last_of(layer) + 2, forward, layer)]

    def turn(now):
        for lag, action in ((0, go_second), (lag_third, go_third), (lag_fourth, go_fourth)):
            begin = max(lag, 1)

            @pl.when(jnp.logical_and(now >= begin, now < chunks + lag))
            def stage():
                action(now - lag)

        for moment, action, *which in timed:

            @pl.when(now == moment)
            def once():
                action(*which)

    loop(chunks + lag_fourth, turn)
    go_head(3)
    arrive(layers - 1)
    forward(layers - 1)
    store(2, 0).start()

    def finish(chunk):
        second(chunk, False).wait_send()
        third(chunk, 0, False).wait_send()
        third(chunk, 1, False).wait_send()
        fourth(chunk, False).wait_send()

    loop(chunks, finish)
    each(1, lambda hop: head_first(hop).wait_send())
    for which in range(3):
        head_next(which, False).wait_send()

    for layer in range(layers):

        each(1, lambda hop: first(layer, hop).wait_send())
        store(0, layer).wait()
        store(1, layer).wait()
    store(2, 0).wait()


def gather_weights(master, head_master, head_width, features, vectors, valid, space_count):
    layers, share, channels = master.shape
    rows, width, unused = features.shape
    deep_count = space_count // 2
    pixels = rows * width
    dims = (layers, rows, width, channels, NH, HD, space_count)
    low, wide_float = jnp.bfloat16, jnp.float32
    anywhere = pl.BlockSpec(memory_space=pl.ANY)
    vmem = pl.BlockSpec(memory_space=pltpu.VMEM)
    head_own = (head_master.shape[0] * LANES // head_width, head_width)
    head_shape = (2, 2, deep_count, 2) + head_own
    wide_shape = (layers, (rows + 2) * width, TAPS * channels)
    full, head_full, wide, hidden, last = pl.pallas_call(
        partial(gather_kernel, dims),
        out_shape=(
            jax.ShapeDtypeStruct((layers, deep_count, 2, share, channels), low),
            jax.ShapeDtypeStruct(head_shape, low),
            jax.ShapeDtypeStruct(wide_shape, low),
            jax.ShapeDtypeStruct((layers, pixels, channels), wide_float),
            jax.ShapeDtypeStruct((pixels, channels), low),
        ),
        in_specs=[vmem] * 4 + [pl.BlockSpec(memory_space=pltpu.SMEM)],
        out_specs=[anywhere] * 5,
        scratch_shapes=[
            pltpu.VMEM(master.shape, low),
            pltpu.VMEM(head_own, low),
            pltpu.VMEM((2, space_count * share, channels), low),
            pltpu.VMEM(wide_shape, low),
            pltpu.VMEM((layers, pixels, channels), wide_float),
            pltpu.VMEM((pixels, channels), low),
            pltpu.VMEM((layers, 2, width, channels), low),
            pltpu.SemaphoreType.DMA((layers + 1,)),
            pltpu.SemaphoreType.DMA((5, layers, deep_count)),
            pltpu.SemaphoreType.DMA((5, layers, deep_count)),
            pltpu.SemaphoreType.DMA((deep_count + 3,)),
            pltpu.SemaphoreType.DMA((deep_count + 3,)),
            pltpu.SemaphoreType.DMA((2, space_count)),
            pltpu.SemaphoreType.DMA((3, layers)),
            pltpu.SemaphoreType.DMA((layers, 2)),
            pltpu.SemaphoreType.DMA((layers, 2)),
        ],
        compiler_params=pltpu.CompilerParams(
            collective_id=0, has_side_effects=True, vmem_limit_bytes=VMEM_LIMIT
        ),
    )(master, head_master, features.reshape(pixels, channels), vectors, valid)
    return (
        full.reshape(layers, space_count * share, channels),
        head_full.reshape(-1, head_width),
        wide,
        hidden,
        last,
    )


def reduce_kernel(
    layers,
    deep_count,
    grads,
    vector,
    total,
    stats,
    vector_total,
    mine,
    core_in,
    second_in,
    kept,
    third_in,
    last,
    last_in,
    acc,
    stat_own,
    stat_in,
    stat_deep,
    vector_out,
    vector_in,
    vector_deep,
    local_sem,
    sends,
    receives,
    stat_sends,
    stat_receives,
    deep_sends,
    deep_receives,
    vector_sends,
    vector_receives,
):
    across, core, deep, side = place()
    block = 2 * core + across
    steps = layers * deep_count

    def split(step):
        layer, hop = step // deep_count, lax.rem(step, deep_count)
        target = lax.rem(deep + hop, deep_count)
        return (layer, hop, target, lax.rem(target, 2))

    def first(step):
        layer, hop, target, odd = split(step)
        return remote(
            grads.at[layer, target, :, :, lanes(2 * (1 - core), 2)],
            core_in.at[step],
            sends.at[0, step],
            receives.at[0, step],
            at(across, 1 - core, deep, side),
        )

    def load(step):
        layer, hop, target, odd = split(step)
        return pltpu.make_async_copy(
            grads.at[layer, target, :, :, lanes(2 * core, 2)], mine.at[step], local_sem.at[step]
        )

    def second(step, half):
        layer, hop, target, odd = split(step)
        piece_side = (1 - odd) * half + odd * (1 - side)
        piece_lane = (1 - odd) * (1 - across) + odd * half
        to = at(lax.rem(across + 1 - odd, 2), core, deep, lax.rem(side + odd, 2))
        return remote(
            mine.at[step, piece_side, :, lanes(piece_lane)],
            second_in.at[step, half],
            sends.at[1 + half, step],
            receives.at[1 + half, step],
            to,
        )

    def third(step):
        layer, hop, target, odd = split(step)
        keep = (1 - odd) * side + odd * across
        to = at(lax.rem(across + odd, 2), core, deep, lax.rem(side + 1 - odd, 2))
        return remote(
            kept.at[step, 1 - keep],
            third_in.at[step],
            sends.at[3, step],
            receives.at[3, step],
            to,
        )

    def fourth(step):
        layer, hop, target, odd = split(step)
        return remote(
            last.at[step],
            last_in.at[step],
            sends.at[4, step],
            receives.at[4, step],
            at(across, core, target, side),
        )

    def fifth(layer, incoming):
        lane = 2 * core + (1 - across if incoming else across)
        piece = total.at[layer, :, lanes(lane)]
        to = at(1 - across, core, deep, side)
        return remote(piece, piece, sends.at[5, layer], receives.at[5, layer], to)

    def sixth(layer, incoming):
        column = 1 - core if incoming else core
        piece = total.at[layer, :, lanes(2 * column, 2)]
        to = at(across, 1 - core, deep, side)
        return remote(piece, piece, sends.at[6, layer], receives.at[6, layer], to)

    def run(low, high, action):
        def body(step, carry):
            action(step)
            return carry

        lax.fori_loop(low, high, body, 0)

    half_block = LANES // 2

    def stat_side(layer, incoming):
        rows = pl.ds(pl.multiple_of((1 - side) * half_block, half_block), half_block)
        return remote(
            stat_own.at[layer, rows],
            stat_in.at[layer],
            stat_sends.at[0, layer],
            stat_receives.at[0, layer],
            at(across, core, deep, 1 - side),
        )

    def stat_along(layer, hop):
        return remote(
            stat_deep.at[layer, deep],
            stat_deep.at[layer, deep],
            deep_sends.at[layer, hop],
            deep_receives.at[layer, hop],
            at(across, core, lax.rem(deep + hop, deep_count), side),
        )

    def stat_along_in(layer, hop):
        source = lax.rem(deep - hop + deep_count, deep_count)
        return remote(
            stat_deep.at[layer, source],
            stat_deep.at[layer, source],
            deep_sends.at[layer, hop],
            deep_receives.at[layer, hop],
            at(across, core, deep, side),
        )

    def half_rows(which):
        return pl.ds(pl.multiple_of(which * half_block, half_block), half_block)

    def stat_spread(which, layer, incoming):
        if which == 0:
            to = at(across, core, deep, 1 - side)
            piece = stats.at[layer, block, half_rows(1 - side if incoming else side)]
        elif which == 1:
            to = at(1 - across, core, deep, side)
            piece = stats.at[layer, 2 * core + (1 - across if incoming else across)]
        else:
            to = at(across, 1 - core, deep, side)
            piece = stats.at[layer, pl.ds(2 * (1 - core if incoming else core), 2)]
        slot = 1 + which
        return remote(piece, piece, stat_sends.at[slot, layer], stat_receives.at[slot, layer], to)

    def vector_step(which):
        to = (
            at(across, 1 - core, deep, side),
            at(1 - across, core, deep, side),
            at(across, core, deep, 1 - side),
        )[which]
        return remote(
            vector_out.at[which],
            vector_in.at[which],
            vector_sends.at[which],
            vector_receives.at[which],
            to,
        )

    def vector_along(hop):
        return remote(
            vector_deep.at[deep],
            vector_deep.at[deep],
            vector_sends.at[2 + hop],
            vector_receives.at[2 + hop],
            at(across, core, lax.rem(deep + hop, deep_count), side),
        )

    def vector_along_in(hop):
        source = lax.rem(deep - hop + deep_count, deep_count)
        return remote(
            vector_deep.at[source],
            vector_deep.at[source],
            vector_sends.at[2 + hop],
            vector_receives.at[2 + hop],
            at(across, core, deep, side),
        )

    def go_first(step):
        load(step).start()
        first(step).start()

    ahead = min(3, steps)
    greet(partners(deep_count))
    run(0, ahead, go_first)

    def wide(left, right):
        return left.astype(jnp.float32) + right.astype(jnp.float32)

    def go_second(step):
        @pl.when(step + ahead < steps)
        def start_next():
            go_first(step + ahead)

        load(step).wait()
        first(step).wait_recv()
        mine[step] = wide(mine[step], core_in[step]).astype(jnp.bfloat16)
        second(step, 0).start()
        second(step, 1).start()

    def go_third(step):
        layer, hop, target, odd = split(step)
        for half in range(2):
            second(step, half).wait_recv()
            keep_side = (1 - odd) * half + odd * side
            keep_lane = (1 - odd) * across + odd * half
            kept[step, half] = wide(
                mine[step, keep_side, :, lanes(keep_lane)], second_in[step, half]
            ).astype(jnp.bfloat16)
        third(step).start()

    def go_fourth(step):
        layer, hop, target, odd = split(step)
        third(step).wait_recv()
        keep = (1 - odd) * side + odd * across
        last[step] = wide(kept[step, keep], third_in[step]).astype(jnp.bfloat16)

        @pl.when(hop > 0)
        def unused():
            fourth(step).start()

    def close(layer):
        acc[...] = last[layer * deep_count].astype(jnp.float32)

        def add(hop):
            step = layer * deep_count + hop
            fourth(step).wait_recv()
            acc[...] += last_in[step].astype(jnp.float32)

        run(1, deep_count, add)
        total[layer, :, lanes(block)] = acc[...].astype(jnp.bfloat16)
        fifth(layer, False).start()

    def spread(layer):
        fifth(layer, True).wait_recv()
        sixth(layer, False).start()

    def measure(layer):
        sixth(layer, True).wait_recv()
        own_lanes = total[layer, :, lanes(block)]
        stat_own[layer] = lax.dot_general(
            own_lanes,
            total[layer],
            (((0,), (0,)), ((), ())),
            preferred_element_type=jnp.float32,
        ).astype(jnp.bfloat16)
        stat_side(layer, False).start()

    def pair(layer):
        stat_side(layer, True).wait_recv()
        stat_deep[layer, deep] = wide(
            stat_own[layer, half_rows(side)], stat_in[layer]
        ).astype(jnp.bfloat16)
        run(1, deep_count, lambda hop: stat_along(layer, hop).start())

    def settle(layer):
        run(1, deep_count, lambda hop: stat_along_in(layer, hop).wait_recv())
        whole = stat_deep[layer, 0].astype(jnp.float32)
        for source in range(1, deep_count):
            whole += stat_deep[layer, source].astype(jnp.float32)
        stats[layer, block, half_rows(side)] = whole.astype(jnp.bfloat16)
        stat_spread(0, layer, False).start()

    def share_across(layer):
        stat_spread(0, layer, True).wait_recv()
        stat_spread(1, layer, False).start()

    def share_core(layer):
        stat_spread(1, layer, True).wait_recv()
        stat_spread(2, layer, False).start()

    def finish(layer):
        stat_spread(2, layer, True).wait_recv()
        fifth(layer, False).wait_send()
        sixth(layer, False).wait_send()
        stat_side(layer, False).wait_send()
        run(1, deep_count, lambda hop: stat_along(layer, hop).wait_send())
        for which in range(3):
            stat_spread(which, layer, False).wait_send()

    def vector_next(which):
        vector_step(which).wait_recv()
        summed = vector_out[which] + vector_in[which]
        if which < 2:
            vector_out[which + 1] = summed
            vector_step(which + 1).start()
        else:
            vector_deep[deep] = summed
            run(1, deep_count, lambda hop: vector_along(hop).start())

    chunk_work = ((0, go_second), (2, go_third), (4, go_fourth))
    layer_work = (
        (6, close),
        (7, spread),
        (8, measure),
        (9, pair),
        (10, settle),
        (11, share_across),
        (12, share_core),
        (13, finish),
    )
    vector_out[0] = vector[...]
    vector_step(0).start()

    def turn(now):
        for lag, action in chunk_work:

            @pl.when(jnp.logical_and(now >= lag, now < steps + lag))
            def chunk():
                action(now - lag)

        for which in range(3):

            @pl.when(now == 2 * which + 1)
            def exchange():
                vector_next(which)

        for lag, action in layer_work:
            past = now - lag - (deep_count - 1)

            @pl.when(
                jnp.logical_and(
                    jnp.logical_and(past >= 0, past < steps), lax.rem(past, deep_count) == 0
                )
            )
            def whole_layer():
                action(past // deep_count)

    run(0, steps + layer_work[-1][0], turn)

    run(1, deep_count, lambda hop: vector_along_in(hop).wait_recv())
    summed = vector_deep[0]
    for source in range(1, deep_count):
        summed += vector_deep[source]
    vector_total[...] = summed
    for which in range(3):
        vector_step(which).wait_send()
    run(1, deep_count, lambda hop: vector_along(hop).wait_send())

    def drain(step):
        layer, hop, target, odd = split(step)
        first(step).wait_send()
        second(step, 0).wait_send()
        second(step, 1).wait_send()
        third(step).wait_send()

        @pl.when(hop > 0)
        def unused():
            fourth(step).wait_send()

    run(0, steps, drain)


def reduce_grads(grads, vector, space_count):
    layers, all_rows, columns = grads.shape
    deep_count, rows = space_count // 2, all_rows // space_count
    steps = layers * deep_count
    low = jnp.bfloat16
    blocks = columns // LANES
    vmem = pl.BlockSpec(memory_space=pltpu.VMEM)
    total, stats, vector_total = pl.pallas_call(
        partial(reduce_kernel, layers, deep_count),
        out_shape=(
            jax.ShapeDtypeStruct((layers, rows, columns), low),
            jax.ShapeDtypeStruct((layers, blocks, LANES, columns), low),
            jax.ShapeDtypeStruct(vector.shape, jnp.float32),
        ),
        in_specs=[pl.BlockSpec(memory_space=pl.ANY), vmem],
        out_specs=[vmem, vmem, vmem],
        scratch_shapes=[
            pltpu.VMEM((steps, 2, rows, 2 * LANES), low),
            pltpu.VMEM((steps, 2, rows, 2 * LANES), low),
            pltpu.VMEM((steps, 2, rows, LANES), low),
            pltpu.VMEM((steps, 2, rows, LANES), low),
            pltpu.VMEM((steps, rows, LANES), low),
            pltpu.VMEM((steps, rows, LANES), low),
            pltpu.VMEM((steps, rows, LANES), low),
            pltpu.VMEM((rows, LANES), jnp.float32),
            pltpu.VMEM((layers, LANES, columns), low),
            pltpu.VMEM((layers, LANES // 2, columns), low),
            pltpu.VMEM((layers, deep_count, LANES // 2, columns), low),
            pltpu.VMEM((3,) + vector.shape, jnp.float32),
            pltpu.VMEM((3,) + vector.shape, jnp.float32),
            pltpu.VMEM((deep_count,) + vector.shape, jnp.float32),
            pltpu.SemaphoreType.DMA((steps,)),
            pltpu.SemaphoreType.DMA((7, steps)),
            pltpu.SemaphoreType.DMA((7, steps)),
            pltpu.SemaphoreType.DMA((4, layers)),
            pltpu.SemaphoreType.DMA((4, layers)),
            pltpu.SemaphoreType.DMA((layers, deep_count)),
            pltpu.SemaphoreType.DMA((layers, deep_count)),
            pltpu.SemaphoreType.DMA((2 + deep_count,)),
            pltpu.SemaphoreType.DMA((2 + deep_count,)),
        ],
        compiler_params=pltpu.CompilerParams(
            collective_id=1, has_side_effects=True, vmem_limit_bytes=VMEM_LIMIT
        ),
    )(grads.reshape(layers, deep_count, 2, rows, columns), vector)
    return (total, stats.reshape(layers, columns, columns), vector_total)


def work_kernel(
    dims,
    weights_in,
    head_in,
    wide_in,
    hidden_in,
    last_in,
    vectors,
    cotangent_in,
    valid,
    merged,
    features_grad,
    grads_out,
    head_grad,
    vector,
    weights,
    head,
    cotangent,
    wide,
    hidden,
    last,
    last_turned,
    d_wide,
    d_active,
    grads,
    halo,
    term,
    term_in,
    load_sem,
    store_sem,
    send_sem,
    receive_sem,
    term_sends,
    term_receives,
    *head_refs,
):
    layers, rows, width, channels, heads, depth, space_count = dims
    deep_count = space_count // 2
    across, core, deep, side = place()
    spread_head = len(head_refs) > 0
    if spread_head:
        head_parts, core_in, across_in, side_in, deep_in, head_sends, head_receives = head_refs
        head_rows = head_parts.shape[4]
    tile = 2 * LANES
    tiles = channels // tile
    low = jnp.bfloat16

    loads = ((last_in, last), (head_in, head), (cotangent_in, cotangent))
    for layer in reversed(range(layers)):
        loads += (
            (hidden_in.at[layer], hidden.at[layer]),
            (wide_in.at[layer], wide.at[layer]),
            (weights_in.at[layer], weights.at[layer]),
        )

    def load(which):
        source, target = loads[which]
        return pltpu.make_async_copy(source, target, load_sem.at[which])

    for which in range(len(loads)):
        load(which).start()

    others = [
        at(across, 1 - core, deep, side),
        at(1 - across, core, deep, side),
        at(across, core, deep, 1 - side),
    ]
    if spread_head:
        others += [
            at(across, core, lax.rem(deep + hop, deep_count), side) for hop in range(1, deep_count)
        ]
    greet_edges(others, space_count)

    def term_lanes(index, which):
        return pl.ds(pl.multiple_of(index * depth + which * LANES, LANES), LANES)

    def term_step(which, index, incoming=False):
        if which == 0:
            source, target, to = term.at[:, term_lanes(index, 1 - core)], term_in.at[0, index], others[0]
        elif which == 1:
            source, target, to = term.at[:, term_lanes(index, core)], term_in.at[1, index], others[1]
        else:
            source = merged.at[:, term_lanes(index, 1 - core if incoming else core)]
            target, to = source, others[0]
        return remote(
            source, target, term_sends.at[which, index], term_receives.at[which, index], to
        )

    def term_pair(index):
        term_step(0, index).wait_recv()
        lane = term_lanes(index, core)
        both = term[:, lane].astype(jnp.float32) + term_in[0, index].astype(jnp.float32)
        term[:, lane] = both.astype(low)
        term_step(1, index).start()

    def term_total(index):
        term_step(1, index).wait_recv()
        lane = term_lanes(index, core)
        both = term[:, lane].astype(jnp.float32) + term_in[1, index].astype(jnp.float32)
        merged[:, lane] = both.astype(low)
        term_step(2, index).start()

    def term_end(index):
        term_step(2, index, True).wait_recv()
        for which in range(3):
            term_step(which, index).wait_send()

    def head_step(which):
        if which == 0:
            source, target, to = head_parts.at[:, 1 - core], core_in, others[0]
        elif which == 1:
            source = head_parts.at[pl.ds(0, 2), core, pl.ds(0, deep_count), 1 - side]
            target, to = side_in, others[2]
        else:
            source = head_parts.at[1 - across, core, pl.ds(0, deep_count), side]
            target, to = across_in, others[1]
        return remote(source, target, head_sends.at[which], head_receives.at[which], to)

    def head_along(hop):
        target = lax.rem(deep + hop, deep_count)
        return remote(
            head_parts.at[across, core, target, side],
            deep_in.at[hop],
            head_sends.at[2 + hop],
            head_receives.at[2 + hop],
            at(across, core, target, side),
        )

    def head_next(which):
        if not spread_head:
            return
        head_step(which).wait_recv()
        if which == 0:
            for part in range(2):
                both = head_parts[part, core].astype(jnp.float32) + core_in[part].astype(jnp.float32)
                head_parts[part, core] = both.astype(low)
            head_step(1).start()
        elif which == 1:
            for part in range(2):
                both = head_parts[part, core, pl.ds(0, deep_count), side].astype(jnp.float32)
                both += side_in[part].astype(jnp.float32)
                head_parts[part, core, pl.ds(0, deep_count), side] = both.astype(low)
            head_step(2).start()
        else:
            both = head_parts[across, core, pl.ds(0, deep_count), side].astype(jnp.float32)
            both += across_in[...].astype(jnp.float32)
            head_parts[across, core, pl.ds(0, deep_count), side] = both.astype(low)
            for hop in range(1, deep_count):
                head_along(hop).start()

    def head_end():
        if not spread_head:
            return
        whole = head_parts[across, core, deep, side].astype(jnp.float32)
        for hop in range(1, deep_count):
            head_along(hop).wait_recv()
            whole += deep_in[hop].astype(jnp.float32)
        blocks = heads * depth // LANES
        for lane in range(blocks):
            head_grad[pl.ds(lane, head_rows, stride=blocks), :] = whole[
                :, lane * LANES : (lane + 1) * LANES
            ]
        for which in range(3):
            head_step(which).wait_send()
        for hop in range(1, deep_count):
            head_along(hop).wait_send()

    send_edges, take_edges, put = edge_tools(dims, halo, send_sem, receive_sem)

    def loop(count, action):
        def body(index, carry):
            action(index)
            return carry

        lax.fori_loop(0, count, body, 0)

    def spot(index):
        return pl.multiple_of(index * tile, tile)

    masks, weights_row = row_weights(valid, rows)

    def put_vector(start, part, value):
        row = start // LANES + 2 * part
        vector[pl.ds(row, 1), :] = value[:, :LANES]
        vector[pl.ds(row + 1, 1), :] = value[:, LANES:]

    pixels = rows * width
    for which in range(3):
        load(which).wait()
    last_turned[...] = last[...].astype(jnp.float32).T.astype(low)
    d_active[...] = jnp.zeros_like(d_active)

    def one_head(index):
        lane = pl.ds(pl.multiple_of(index * depth, depth), depth)
        projected = mix(last[...], head[:, lane], 1, 0)
        projected += vector_lanes(vectors, layers * channels, index)
        gain = vector_lanes(vectors, layers * channels + heads * depth, index)
        gain_total = jnp.zeros((1, depth), jnp.float32)
        bias_total = jnp.zeros((1, depth), jnp.float32)
        rounded = []
        for row in range(rows):
            span = slice(row * width, (row + 1) * width)
            weight = weights_row[row]
            value = projected[span]
            inverse = lax.rsqrt(jnp.sum(value * value, -1, keepdims=True) + 1e-06)
            normed = value * inverse
            scaled = gain * weight
            term[span, lane] = (normed * scaled).astype(low)
            given = cotangent[span, lane].astype(jnp.float32)
            gain_total += jnp.sum(normed * given, 0, keepdims=True) * weight
            d_normed = given * scaled
            along = jnp.sum(normed * d_normed, -1, keepdims=True)
            d_low = (inverse * (d_normed - normed * along)).astype(low)
            bias_total += jnp.sum(d_low.astype(jnp.float32), 0, keepdims=True)
            rounded.append(d_low)
        term_step(0, index).start()
        put_vector(layers * channels + heads * depth, index, gain_total)
        put_vector(layers * channels, index, bias_total)
        d_low = jnp.concatenate(rounded, 0)
        grad = mix(last_turned[...], d_low, 1, 0)
        if spread_head:
            split = grad.reshape(2, 2, deep_count, 2, head_rows, depth)
            head_parts[:, :, :, :, :, lane] = split.astype(low)
        else:
            head_grad[:, lane] = grad.astype(low)
        d_active[...] += mix(d_low, head[:, lane], 1, 1)

        @pl.when(index > 0)
        def earlier():
            term_pair(index - 1)

    loop(heads, one_head)
    if spread_head:
        head_step(0).start()
    term_pair(heads - 1)

    def store(layer):
        slot = layer % 2
        return pltpu.make_async_copy(grads.at[slot], grads_out.at[layer], store_sem.at[slot])

    for layer in reversed(range(layers)):
        which = layers - 1 - layer
        for part in range(3):
            load(3 + 3 * which + part).wait()

        def enter(part):
            lane = pl.ds(spot(part), tile)
            total = jnp.zeros((1, tile), jnp.float32)
            for row in range(rows):
                span = slice(row * width, (row + 1) * width)
                slope = gelu_slope(hidden[layer, span, lane])
                value = slope * (masks[row] * d_active[span, lane])
                value = value.astype(low).astype(jnp.float32)
                total += jnp.sum(value, 0, keepdims=True)
                put(d_wide, row + 1, spot(part), tile, value)
            put_vector(layer * channels, part, total)

        loop(tiles, enter)
        send_edges(which, d_wide)
        if layer + 2 < layers:
            store(layer + 2).wait()

        def one_tap(tap):
            tap_row, tap_column = tap // TAPS, lax.rem(tap, TAPS)
            window = wide[
                layer,
                pl.ds(pl.multiple_of(tap_row * width, width), pixels),
                pl.ds(pl.multiple_of(tap_column * channels, channels), channels),
            ]
            d_hidden = d_wide[width : width + pixels, channels : 2 * channels]
            grads[layer % 2, pl.ds(pl.multiple_of(tap * channels, channels), channels), :] = mix(
                window, d_hidden, 0, 0
            ).astype(low)

        loop(TAPS * TAPS, one_tap)
        store(layer).start()
        head_next(layers - 1 - layer)
        take_edges(which, d_wide)

        def back(part):
            total = jnp.zeros((pixels, tile), jnp.float32)
            for tap_row in range(TAPS):
                for tap_column in range(TAPS):
                    window = d_wide[
                        (2 - tap_row) * width : (2 - tap_row) * width + pixels,
                        (2 - tap_column) * channels : (3 - tap_column) * channels,
                    ]
                    first = (TAPS * tap_row + tap_column) * channels
                    total += mix(
                        window, weights[layer, pl.ds(first + spot(part), tile), :], 1, 1
                    )
            d_active[:, pl.ds(spot(part), tile)] = total

        loop(tiles, back)

    loop(heads, term_total)
    features_grad[...] = d_active[...].astype(low)
    head_end()
    loop(heads, term_end)
    for layer in range(min(layers, 2)):
        store(layer).wait()


def run_block(
    weights, head, wide, hidden, last, vectors, cotangent, valid, space_count
):
    rows, width, unused = cotangent.shape
    layers, unused, channels = weights.shape
    head_width = head.shape[1]
    pixels = rows * width
    deep_count = space_count // 2
    head_rows = channels // (4 * space_count)
    spread_head = head_rows % 16 == 0
    low, full = jnp.bfloat16, jnp.float32
    dims = (layers, rows, width, channels, NH, HD, space_count)
    vmem = pl.BlockSpec(memory_space=pltpu.VMEM)
    anywhere = pl.BlockSpec(memory_space=pl.ANY)
    head_scratch = []
    head_out = jax.ShapeDtypeStruct((channels, head_width), low)
    if spread_head:
        head_out = jax.ShapeDtypeStruct((head_rows * head_width // LANES, LANES), full)
        head_scratch = [
            pltpu.VMEM((2, 2, deep_count, 2, head_rows, head_width), low),
            pltpu.VMEM((2, deep_count, 2, head_rows, head_width), low),
            pltpu.VMEM((deep_count, head_rows, head_width), low),
            pltpu.VMEM((2, deep_count, head_rows, head_width), low),
            pltpu.VMEM((deep_count, head_rows, head_width), low),
            pltpu.SemaphoreType.DMA((2 + deep_count,)),
            pltpu.SemaphoreType.DMA((2 + deep_count,)),
        ]
    outs = pl.pallas_call(
        partial(work_kernel, dims),
        out_shape=(
            jax.ShapeDtypeStruct((pixels, head_width), low),
            jax.ShapeDtypeStruct((pixels, channels), low),
            jax.ShapeDtypeStruct(weights.shape, low),
            head_out,
            jax.ShapeDtypeStruct(vectors.shape, full),
        ),
        in_specs=[
            anywhere,
            anywhere,
            anywhere,
            anywhere,
            anywhere,
            vmem,
            anywhere,
            pl.BlockSpec(memory_space=pltpu.SMEM),
        ],
        out_specs=[vmem, vmem, anywhere, vmem, vmem],
        scratch_shapes=[
            pltpu.VMEM(weights.shape, low),
            pltpu.VMEM(head.shape, low),
            pltpu.VMEM((pixels, head_width), low),
            pltpu.VMEM((layers, (rows + 2) * width, TAPS * channels), low),
            pltpu.VMEM((layers, pixels, channels), full),
            pltpu.VMEM((pixels, channels), low),
            pltpu.VMEM((channels, pixels), low),
            pltpu.VMEM(((rows + 2) * width, TAPS * channels), low),
            pltpu.VMEM((pixels, channels), full),
            pltpu.VMEM((2,) + weights.shape[1:], low),
            pltpu.VMEM((layers, 2, width, channels), low),
            pltpu.VMEM((pixels, head_width), low),
            pltpu.VMEM((2, NH, pixels, LANES), low),
            pltpu.SemaphoreType.DMA((3 * layers + 3,)),
            pltpu.SemaphoreType.DMA((2,)),
            pltpu.SemaphoreType.DMA((layers, 2)),
            pltpu.SemaphoreType.DMA((layers, 2)),
            pltpu.SemaphoreType.DMA((3, NH)),
            pltpu.SemaphoreType.DMA((3, NH)),
        ]
        + head_scratch,
        compiler_params=pltpu.CompilerParams(
            collective_id=2, has_side_effects=True, vmem_limit_bytes=VMEM_LIMIT
        ),
    )(
        weights,
        head,
        wide,
        hidden,
        last,
        vectors,
        cotangent.reshape(pixels, head_width),
        valid,
    )
    merged, features_grad, grads, head_grad, vector = outs
    if not spread_head:
        head_grad = lax.psum_scatter(
            head_grad.astype(full).reshape(-1), ("scale", "space"), scatter_dimension=0, tiled=True
        ).reshape(-1, LANES)
    return (merged, features_grad, grads, head_grad, vector)


def halves(value):
    high = value.astype(jnp.bfloat16)
    return (high, (value - high.astype(jnp.float32)).astype(jnp.bfloat16))


def dot(left, right, left_dim, right_dim):
    left_high, left_low = halves(left)
    right_high, right_low = halves(right)
    rest = mix(left_high, right_low, left_dim, right_dim) + mix(left_low, right_high, left_dim, right_dim)
    return mix(left_high, right_high, left_dim, right_dim) + rest


def quick(x):
    return pl.reciprocal(x,approx=True)
def eliminate(blocks, off, size, m=8):
    nl=len(blocks); nb=size//8; W=blocks[0][0].shape[1]
    sub=lax.broadcasted_iota(jnp.int32,(8,128),0)
    for k0 in range(0,size,m):
        b0=k0//8; s0=k0%8
        for l in range(nl):
            bl=blocks[l]
            top=bl[b0]
            def colb(b,j):
                return jnp.broadcast_to(bl[b][:,off+k0+j:off+k0+j+1],(8,128))
            c0=[colb(b0,j) for j in range(m)]
            a=[[None]*m for _ in range(m)]
            for j in range(m):
                for i in range(j,m):
                    a[i][j]=jnp.broadcast_to(c0[j][s0+i:s0+i+1,:],(8,128))
            inv=[]; low=[[None]*m for _ in range(m)]
            for k in range(m):
                r=quick(a[k][k]); inv.append(r)
                for i in range(k+1,m):
                    low[i][k]=a[i][k]*r
                for j in range(k+1,m):
                    for i in range(j,m):
                        a[i][j]=a[i][j]-low[i][k]*a[j][k]
            wid=lambda v: jnp.concatenate([v]*(W//128),1)
            rows=[jnp.broadcast_to(top[s0+i:s0+i+1,:],(8,W)) for i in range(m)]
            for i in range(m):
                for k in range(i):
                    rows[i]=rows[i]-wid(low[i][k])*rows[k]
            for b in range(b0,nb):
                if b==b0 and s0+m==8 and m==1: continue
                cs=list(c0) if b==b0 else [colb(b,j) for j in range(m)]
                for j in range(m):
                    for k in range(j):
                        cs[j]=cs[j]-low[j][k]*cs[k]
                acc=bl[b]
                for k in range(m):
                    w=cs[k]*inv[k]
                    if b==b0: w=jnp.where(sub>s0+k,w,0.0)
                    acc=acc-wid(w)*rows[k]
                bl[b]=acc
    out=[]
    lane=lax.broadcasted_iota(jnp.int32,(8,W),1)
    row8=lax.broadcasted_iota(jnp.int32,(8,W),0)
    for l in range(nl):
        res=[]
        for b in range(nb):
            v=blocks[l][b]
            d=jnp.sum(jnp.where(lane==row8+(off+8*b),v,0.0),1,keepdims=True)
            res.append(v*lax.rsqrt(d))
        out.append(jnp.concatenate(res,0))
    return out


def moments(grads, first, second):
    first_new = BETA_ONE * first + (1.0 - BETA_ONE) * grads
    second_new = BETA_TWO * second + (1.0 - BETA_TWO) * grads * grads
    direction = (
        first_new
        * (1.0 / (1.0 - BETA_ONE**STEP))
        / (jnp.sqrt(second_new * (1.0 / (1.0 - BETA_TWO**STEP))) + EPSILON)
    )
    return (first_new, second_new, direction)


def update_kernel(
    dims,
    summed,
    statistics,
    bases,
    grads,
    first_in,
    second_in,
    master_in,
    head_grad,
    head_first,
    head_second,
    head_master,
    vector_grad,
    vector_first,
    vector_second,
    vectors,
    stats_new,
    bases_new,
    first_out,
    second_out,
    master_out,
    head_first_new,
    head_second_new,
    head_new,
    vector_first_new,
    vector_second_new,
    vectors_new,
    system,
    pivot,
    first,
    second,
    master,
    load_sem,
    store_sem,
):
    layers, rows, channels, piece, bias_rows, panel = dims
    block = LANES

    def load(which, layer):
        source, target = ((first_in, first), (second_in, second), (master_in, master))[which]
        return pltpu.make_async_copy(
            source.at[layer], target.at[layer], load_sem.at[which, layer]
        )

    def store(which, layer):
        source, target = ((first, first_out), (second, second_out), (master, master_out))[which]
        return pltpu.make_async_copy(
            source.at[layer], target.at[layer], store_sem.at[which, layer]
        )

    for layer in range(layers):
        for which in range(3):
            load(which, layer).start()

    for layer in range(layers):
        fresh = BETA_TWO * statistics[layer] + (1.0 - BETA_TWO) * summed[layer].astype(jnp.float32)
        stats_new[layer] = fresh
        turned = dot(bases[layer], fresh, 0, 0)
        system[layer, :, channels : 2 * channels] = turned
        system[layer, :, 0:channels] = dot(turned, turned, 1, 1)

    head = moments(head_grad[...], head_first[...], head_second[...])
    head_first_new[...] = head[0]
    head_second_new[...] = head[1]
    head_new[...] = head_master[...] - RATE_HEAD * (head[2] + DECAY * head_master[...])
    vec = moments(vector_grad[...], vector_first[...], vector_second[...])
    vector_first_new[...] = vec[0]
    vector_second_new[...] = vec[1]
    row = lax.broadcasted_iota(jnp.int32, vectors.shape, 0)
    rates = jnp.where(row < bias_rows, RATE_BIAS, RATE_GAIN)
    vectors_new[...] = vectors[...] - rates * (vec[2] + DECAY * vectors[...])

    for layer in range(layers):
        for which in range(3):
            load(which, layer).wait()
        high, rest = halves(bases[layer])

        def one_piece(index, carry):
            here = pl.ds(pl.multiple_of(index * piece, piece), piece)
            given = grads[layer, here, :]
            rotated = mix(given, high, 1, 0) + mix(given, rest, 1, 0)
            first_new, second_new, direction = moments(
                rotated, first[layer, here, :], second[layer, here, :]
            )
            first[layer, here, :] = first_new
            second[layer, here, :] = second_new
            up, down = halves(direction)
            back = mix(up, high, 1, 1) + (mix(up, rest, 1, 1) + mix(down, high, 1, 1))
            old = master[layer, here, :]
            master[layer, here, :] = old - RATE_CONV * (back + DECAY * old)
            return carry

        lax.fori_loop(0, rows // piece, one_piece, 0)
        for which in range(3):
            store(which, layer).start()

    eye = (
        lax.broadcasted_iota(jnp.int32, (block, block), 0)
        == lax.broadcasted_iota(jnp.int32, (block, block), 1)
    ).astype(jnp.float32)

    def outer(k, carry):
        here = pl.ds(pl.multiple_of(k * block, block), block)
        panels = [jnp.concatenate([system[layer, here, here], eye], 1) for layer in range(layers)]
        done = [[] for _ in range(layers)]
        for j in range(block // panel):
            blocks = [[p[8 * i : 8 * i + 8] for i in range(panel // 8)] for p in panels]
            tops = eliminate(blocks, panel * j, panel)
            for layer in range(layers):
                done[layer].append(tops[layer][:, block:])
                if j < block // panel - 1:
                    panels[layer] = panels[layer][panel:] - dot(
                        tops[layer][:, panel * (j + 1) : block], tops[layer], 0, 0
                    )
        for layer in range(layers):
            inverse = jnp.concatenate(done[layer], 0)
            pivot[layer] = dot(inverse, system[layer, here, :], 1, 0)
            system[layer, here, channels : 2 * channels] = pivot[layer, :, channels : 2 * channels]

        def inner(i, carry_in):
            below = pl.ds(pl.multiple_of(i * block, block), block)
            for layer in range(layers):
                system[layer, below, :] -= dot(pivot[layer, :, below], pivot[layer], 0, 0)
            return carry_in

        lax.fori_loop(k + 1, channels // block, inner, 0)
        return carry

    lax.fori_loop(0, channels // block, outer, 0)
    for layer in range(layers):
        bases_new[layer] = system[layer, :, channels : 2 * channels].T
        for which in range(3):
            store(which, layer).wait()


def update(summed, statistics, bases, grads, conv, head, vector, bias_rows):
    layers, rows, channels = grads.shape
    piece = 144 if rows % 144 == 0 else rows
    dims = (layers, rows, channels, piece, bias_rows, 32)
    vmem = pl.BlockSpec(memory_space=pltpu.VMEM)
    anywhere = pl.BlockSpec(memory_space=pl.ANY)
    square = jax.ShapeDtypeStruct(statistics.shape, jnp.float32)
    tall = jax.ShapeDtypeStruct(grads.shape, jnp.float32)
    head_shape = jax.ShapeDtypeStruct(head[0].shape, jnp.float32)
    vector_shape = jax.ShapeDtypeStruct(vector[0].shape, jnp.float32)
    return pl.pallas_call(
        partial(update_kernel, dims),
        out_shape=(square,) * 2 + (tall,) * 3 + (head_shape,) * 3 + (vector_shape,) * 3,
        in_specs=[vmem] * 4 + [anywhere] * 3 + [vmem] * 8,
        out_specs=[vmem] * 2 + [anywhere] * 3 + [vmem] * 6,
        scratch_shapes=[
            pltpu.VMEM((layers, channels, 2 * channels), jnp.float32),
            pltpu.VMEM((layers, LANES, 2 * channels), jnp.float32),
            pltpu.VMEM(grads.shape, jnp.float32),
            pltpu.VMEM(grads.shape, jnp.float32),
            pltpu.VMEM(grads.shape, jnp.float32),
            pltpu.SemaphoreType.DMA((3, layers)),
            pltpu.SemaphoreType.DMA((3, layers)),
        ],
        compiler_params=pltpu.CompilerParams(vmem_limit_bytes=VMEM_LIMIT),
    )(summed, statistics, bases, grads, *conv, *head, *vector)


def local(
    features,
    valid_rows,
    conv_master,
    head_master,
    vectors,
    conv_first,
    conv_second,
    head_first,
    head_second,
    vec_first,
    vec_second,
    statistics,
    bases,
    cotangent,
):
    channels = features.shape[3]
    head_width = cotangent.shape[2]
    space_count = lax.axis_size("space")
    vectors, vec_first, vec_second, head_master, head_first, head_second = (
        array.reshape(-1, LANES)
        for array in (vectors, vec_first, vec_second, head_master, head_first, head_second)
    )
    conv_used, head_used, wide, hidden, last = gather_weights(
        conv_master, head_master, head_width, features[0], vectors, valid_rows, space_count
    )
    merged, features_grad, grads, owned_head, vector = run_block(
        conv_used,
        head_used,
        wide,
        hidden,
        last,
        vectors,
        cotangent,
        valid_rows,
        space_count,
    )
    owned_conv, summed_stats, grad_vec = reduce_grads(grads, vector, space_count)
    outs = update(
        summed_stats,
        statistics,
        bases,
        owned_conv,
        (conv_first, conv_second, conv_master),
        (owned_head, head_first, head_second, head_master),
        (grad_vec, vec_first, vec_second, vectors),
        (3 * channels + head_width) // LANES,
    )
    stats_new, bases_new = outs[:2]
    return (
        merged.reshape(cotangent.shape),
        features_grad.reshape(features.shape),
        *outs[2:5],
        *(out.reshape(-1) for out in outs[5:]),
        stats_new,
        bases_new,
    )


def solution(mesh):
    in_specs = (
        P("scale", "space", None, None),
        P(),
        P(None, "space", None),
        P(("scale", "space")),
        P(),
        P(None, "space", None),
        P(None, "space", None),
        P(("scale", "space")),
        P(("scale", "space")),
        P(),
        P(),
        P(),
        P(),
        P("space", None, None),
    )
    out_specs = (
        P("space", None, None),
        P("scale", "space", None, None),
        P(None, "space", None),
        P(None, "space", None),
        P(None, "space", None),
        P(("scale", "space")),
        P(("scale", "space")),
        P(("scale", "space")),
        P(),
        P(),
        P(),
        P(),
        P(),
    )
    return jax.shard_map(local, mesh=mesh, in_specs=in_specs, out_specs=out_specs, check_vma=False)
```

profile of v0, /device:TPU:0, one launch (start us, length us, event | category | flops | bytes accessed | tf_op | source)
XLA Modules:
  0.0 330.1 jit_solution(6406526241612393837)
XLA Ops:
  0.6 96.7 %shard_map.237 = (bf16[3,4,2,576,512]{4,3,2,1,0:T(8,128)(2,1)}, bf16[2,2,4,2,16,1792]{5,4,3,2,1,0:T(8,128)(2,1)}, bf16[3,768,1536]{2,1,0:T(8,128)(2,1)}, f32[3,512,512]{2,1,0:T(8,128)}, bf16[512,512]{1,0:T(8,128)(2,1)}) custom-call(f32[3,576,512]{2,1,0:T(8,128)} %master_in.1, f32[224,128]{1,0:T(8,128)} %bitcast.28, bf16[512,512]{1,0:T(8,128)(2,1)} %bitcast.26, ...), custom_call_target="tpu_custom_call" | custom-call | tf_op jit(solution)/shard_map/pallas_call | solution.py:537
  97.4 54.8 %shard_map.238 = (bf16[512,1792]{1,0:T(8,128)(2,1)}, bf16[512,512]{1,0:T(8,128)(2,1)}, bf16[3,4608,512]{2,1,0:T(8,128)(2,1)}, f32[224,128]{1,0:T(8,128)}, f32[40,128]{1,0:T(8,128)}) custom-call(bf16[3,4608,512]{2,1,0:T(8,128)(2,1)} %bitcast.21, bf16[512,1792]{1,0:T(8,128)(2,1)} %bitcast.24, bf16[3,768,1536]{2,1,0:T(8,128)(2,1)} %get-tuple-element.39.wide_in, ...), custom_call_target="tpu_custom_call" | custom-call | tf_op jit(solution)/shard_map/pallas_call | solution.py:1323
  152.2 114.1 %shard_map.239 = (bf16[3,576,512]{2,1,0:T(8,128)(2,1)}, bf16[3,4,128,512]{3,2,1,0:T(8,128)(2,1)}, f32[40,128]{1,0:T(8,128)}) custom-call(bf16[3,4,2,576,512]{4,3,2,1,0:T(8,128)(2,1)} %bitcast.20, f32[40,128]{1,0:T(8,128)} %get-tuple-element.45.vector), custom_call_target="tpu_custom_call" | custom-call | tf_op jit(solution)/shard_map/pallas_call | solution.py:952
  266.3 0.0 copy-start
  266.3 61.6 %shard_map.240 = (f32[3,512,512]{2,1,0:T(8,128)}, f32[3,512,512]{2,1,0:T(8,128)}, f32[3,576,512]{2,1,0:T(8,128)}, f32[3,576,512]{2,1,0:T(8,128)}, f32[3,576,512]...) custom-call(bf16[3,512,512]{2,1,0:T(8,128)(2,1)} %bitcast.25, ...), custom_call_target="tpu_custom_call" | custom-call | tf_op jit(solution)/shard_map/pallas_call | solution.py:1610
  328.0 0.0 copy-start.1
  328.0 0.0 copy-done
  328.0 1.2 copy.29
  329.2 0.1 copy-done.1
  329.3 0.8 copy.30
Async XLA Ops:
  266.3 61.7 %copy-start = (bf16[512,1792]{1,0:T(8,128)(2,1)S(1)}, bf16[512,1792]{1,0:T(8,128)(2,1)}, u32[]{:S(2)}) copy-start(bf16[512,1792]{1,0:T(8,128)(2,1)} %get-tuple-element.42) | copy-start | bytes 5505028
  328.0 1.3 copy-start.1
where the time goes:
time: 331 us; the launch traced here: 330 us
  Pallas kernels  327 us (99%)
    pallas_call x1, Pallas kernels, reduce_grads(): pl.pallas_call(partial(reduce_kernel, layers, deep_count), out_shape=(jax...  114 us
    pallas_call x1, Pallas kernels, gather_weights(): pl.pallas_call(partial(gather_kernel, dims), out_shape=(jax.ShapeDtypeStr...  96.7 us
    pallas_call x1, Pallas kernels, update(): pl.pallas_call(partial(update_kernel, dims), out_shape=(square,) * 2 + (t...  61.6 us
    pallas_call x1, Pallas kernels, run_block(): pl.pallas_call(partial(work_kernel, dims), out_shape=(jax.ShapeDtypeStruc...  54.8 us

commit v1 on v0

--- a/solution.py
+++ b/solution.py
@@ -581,9 +581,16 @@
     deep_count,
     grads,
     vector,
+    bases,
+    first_in,
+    second_moment_in,
+    master_in,
     total,
     stats,
     vector_total,
+    first_out,
+    second_out,
+    master_out,
     mine,
     core_in,
     second_in,
@@ -598,6 +605,9 @@
     vector_out,
     vector_in,
     vector_deep,
+    moment_one,
+    moment_two,
+    master,
     local_sem,
     sends,
     receives,
@@ -607,13 +617,15 @@
     deep_receives,
     vector_sends,
     vector_receives,
+    state_loads,
+    state_stores,
 ):
     across, core, deep, side = place()
     block = 2 * core + across
     steps = layers * deep_count
 
     def split(step):
-        layer, hop = step // deep_count, lax.rem(step, deep_count)
+        layer, hop = step // deep_count, lax.rem(step + 1, deep_count)
         target = lax.rem(deep + hop, deep_count)
         return (layer, hop, target, lax.rem(target, 2))
 
@@ -722,12 +734,14 @@
         return pl.ds(pl.multiple_of(which * half_block, half_block), half_block)
 
     def stat_spread(which, layer, incoming):
-        if which == 0:
-            to = at(across, core, deep, 1 - side)
-            piece = stats.at[layer, block, half_rows(1 - side if incoming else side)]
-        elif which == 1:
-            to = at(1 - across, core, deep, side)
-            piece = stats.at[layer, 2 * core + (1 - across if incoming else across)]
+        if which < 3:
+            other_side = side if which == 1 else 1 - side
+            other_across = across if which == 0 else 1 - across
+            to = at(other_across, core, deep, other_side)
+            if incoming:
+                piece = stats.at[layer, 2 * core + other_across, half_rows(other_side)]
+            else:
+                piece = stats.at[layer, block, half_rows(side)]
         else:
             to = at(across, 1 - core, deep, side)
             piece = stats.at[layer, pl.ds(2 * (1 - core if incoming else core), 2)]
@@ -772,8 +786,30 @@
         first(step).start()
 
     ahead = min(3, steps)
-    greet(partners(deep_count))
+    piece_rows = 144 if total.shape[1] % 144 == 0 else total.shape[1]
+    states = (
+        (first_in, moment_one, first_out),
+        (second_moment_in, moment_two, second_out),
+        (master_in, master, master_out),
+    )
+
+    def load_state(which, layer):
+        source, target, unused = states[which]
+        return pltpu.make_async_copy(
+            source.at[layer], target.at[layer], state_loads.at[which, layer]
+        )
+
+    def store_state(which, layer):
+        unused, source, target = states[which]
+        return pltpu.make_async_copy(
+            source.at[layer], target.at[layer], state_stores.at[which, layer]
+        )
+
+    greet(partners(deep_count) + [at(1 - across, core, deep, 1 - side)])
     run(0, ahead, go_first)
+    for layer in range(layers):
+        for which in range(3):
+            load_state(which, layer).start()
 
     def wide(left, right):
         return left.astype(jnp.float32) + right.astype(jnp.float32)
@@ -811,10 +847,10 @@
             fourth(step).start()
 
     def close(layer):
-        acc[...] = last[layer * deep_count].astype(jnp.float32)
+        acc[...] = last[layer * deep_count + deep_count - 1].astype(jnp.float32)
 
         def add(hop):
-            step = layer * deep_count + hop
+            step = layer * deep_count + hop - 1
             fourth(step).wait_recv()
             acc[...] += last_in[step].astype(jnp.float32)
 
@@ -850,24 +886,47 @@
         for source in range(1, deep_count):
             whole += stat_deep[layer, source].astype(jnp.float32)
         stats[layer, block, half_rows(side)] = whole.astype(jnp.bfloat16)
-        stat_spread(0, layer, False).start()
-
-    def share_across(layer):
-        stat_spread(0, layer, True).wait_recv()
-        stat_spread(1, layer, False).start()
+        for which in range(3):
+            stat_spread(which, layer, False).start()
 
     def share_core(layer):
-        stat_spread(1, layer, True).wait_recv()
-        stat_spread(2, layer, False).start()
+        for which in range(3):
+            stat_spread(which, layer, True).wait_recv()
+        stat_spread(3, layer, False).start()
+
+    def refresh(layer):
+        for which in range(3):
+            load_state(which, layer).wait()
+        high, rest = halves(bases[layer])
+
+        def one_piece(index):
+            here = pl.ds(pl.multiple_of(index * piece_rows, piece_rows), piece_rows)
+            given = total[layer, here, :]
+            rotated = mix(given, high, 1, 0) + mix(given, rest, 1, 0)
+            first_new, second_new, direction = moments(
+                rotated, moment_one[layer, here, :], moment_two[layer, here, :]
+            )
+            moment_one[layer, here, :] = first_new
+            moment_two[layer, here, :] = second_new
+            up, down = halves(direction)
+            back = mix(up, high, 1, 1) + (mix(up, rest, 1, 1) + mix(down, high, 1, 1))
+            old = master[layer, here, :]
+            master[layer, here, :] = old - RATE_CONV * (back + DECAY * old)
+
+        run(0, total.shape[1] // piece_rows, one_piece)
+        for which in range(3):
+            store_state(which, layer).start()
 
     def finish(layer):
-        stat_spread(2, layer, True).wait_recv()
+        stat_spread(3, layer, True).wait_recv()
         fifth(layer, False).wait_send()
         sixth(layer, False).wait_send()
         stat_side(layer, False).wait_send()
         run(1, deep_count, lambda hop: stat_along(layer, hop).wait_send())
+        for which in range(4):
+            stat_spread(which, layer, False).wait_send()
         for which in range(3):
-            stat_spread(which, layer, False).wait_send()
+            store_state(which, layer).wait()
 
     def vector_next(which):
         vector_step(which).wait_recv()
@@ -885,8 +944,8 @@
         (7, spread),
         (8, measure),
         (9, pair),
-        (10, settle),
-        (11, share_across),
+        (10, refresh),
+        (11, settle),
         (12, share_core),
         (13, finish),
     )
@@ -942,22 +1001,27 @@
     run(0, steps, drain)
 
 
-def reduce_grads(grads, vector, space_count):
+def reduce_grads(grads, vector, bases, conv, space_count):
     layers, all_rows, columns = grads.shape
     deep_count, rows = space_count // 2, all_rows // space_count
     steps = layers * deep_count
     low = jnp.bfloat16
     blocks = columns // LANES
     vmem = pl.BlockSpec(memory_space=pltpu.VMEM)
-    total, stats, vector_total = pl.pallas_call(
+    tall = jax.ShapeDtypeStruct((layers, rows, columns), jnp.float32)
+    anywhere = pl.BlockSpec(memory_space=pl.ANY)
+    total, stats, vector_total, *conv_new = pl.pallas_call(
         partial(reduce_kernel, layers, deep_count),
         out_shape=(
             jax.ShapeDtypeStruct((layers, rows, columns), low),
             jax.ShapeDtypeStruct((layers, blocks, LANES, columns), low),
             jax.ShapeDtypeStruct(vector.shape, jnp.float32),
+            tall,
+            tall,
+            tall,
         ),
-        in_specs=[pl.BlockSpec(memory_space=pl.ANY), vmem],
-        out_specs=[vmem, vmem, vmem],
+        in_specs=[anywhere, vmem, vmem] + [anywhere] * 3,
+        out_specs=[vmem] * 3 + [anywhere] * 3,
         scratch_shapes=[
             pltpu.VMEM((steps, 2, rows, 2 * LANES), low),
             pltpu.VMEM((steps, 2, rows, 2 * LANES), low),
@@ -973,21 +1037,26 @@
             pltpu.VMEM((3,) + vector.shape, jnp.float32),
             pltpu.VMEM((3,) + vector.shape, jnp.float32),
             pltpu.VMEM((deep_count,) + vector.shape, jnp.float32),
+            pltpu.VMEM(tall.shape, jnp.float32),
+            pltpu.VMEM(tall.shape, jnp.float32),
+            pltpu.VMEM(tall.shape, jnp.float32),
             pltpu.SemaphoreType.DMA((steps,)),
             pltpu.SemaphoreType.DMA((7, steps)),
             pltpu.SemaphoreType.DMA((7, steps)),
-            pltpu.SemaphoreType.DMA((4, layers)),
-            pltpu.SemaphoreType.DMA((4, layers)),
+            pltpu.SemaphoreType.DMA((5, layers)),
+            pltpu.SemaphoreType.DMA((5, layers)),
             pltpu.SemaphoreType.DMA((layers, deep_count)),
             pltpu.SemaphoreType.DMA((layers, deep_count)),
             pltpu.SemaphoreType.DMA((2 + deep_count,)),
             pltpu.SemaphoreType.DMA((2 + deep_count,)),
+            pltpu.SemaphoreType.DMA((3, layers)),
+            pltpu.SemaphoreType.DMA((3, layers)),
         ],
         compiler_params=pltpu.CompilerParams(
             collective_id=1, has_side_effects=True, vmem_limit_bytes=VMEM_LIMIT
         ),
-    )(grads.reshape(layers, deep_count, 2, rows, columns), vector)
-    return (total, stats.reshape(layers, columns, columns), vector_total)
+    )(grads.reshape(layers, deep_count, 2, rows, columns), vector, bases, *conv)
+    return (stats.reshape(layers, columns, columns), vector_total, conv_new)
 
 
 def work_kernel(
@@ -1463,13 +1532,25 @@
 
 def update_kernel(
     dims,
+    *refs,
+):
+    moved = dims[4]
+    inputs, outputs = refs[: moved + 11], refs[moved + 11 : -1 - moved]
+    held = refs[-1 - moved : -1]
+    update_body(
+        dims, inputs[:moved], outputs[:moved], held, refs[-1], *inputs[moved:], *outputs[moved:]
+    )
+
+
+def update_body(
+    dims,
+    moved_in,
+    moved_out,
+    held,
+    moved_sem,
     summed,
     statistics,
     bases,
-    grads,
-    first_in,
-    second_in,
-    master_in,
     head_grad,
     head_first,
     head_second,
@@ -1480,9 +1561,6 @@
     vectors,
     stats_new,
     bases_new,
-    first_out,
-    second_out,
-    master_out,
     head_first_new,
     head_second_new,
     head_new,
@@ -1491,30 +1569,18 @@
     vectors_new,
     system,
     pivot,
-    first,
-    second,
-    master,
-    load_sem,
-    store_sem,
 ):
-    layers, rows, channels, piece, bias_rows, panel = dims
+    layers, channels, bias_rows, panel, moved = dims
     block = LANES
 
-    def load(which, layer):
-        source, target = ((first_in, first), (second_in, second), (master_in, master))[which]
-        return pltpu.make_async_copy(
-            source.at[layer], target.at[layer], load_sem.at[which, layer]
-        )
-
-    def store(which, layer):
-        source, target = ((first, first_out), (second, second_out), (master, master_out))[which]
-        return pltpu.make_async_copy(
-            source.at[layer], target.at[layer], store_sem.at[which, layer]
-        )
-
-    for layer in range(layers):
-        for which in range(3):
-            load(which, layer).start()
+    def take(which):
+        return pltpu.make_async_copy(moved_in[which], held[which], moved_sem.at[0, which])
+
+    def give(which):
+        return pltpu.make_async_copy(held[which], moved_out[which], moved_sem.at[1, which])
+
+    for which in range(moved):
+        take(which).start()
 
     for layer in range(layers):
         fresh = BETA_TWO * statistics[layer] + (1.0 - BETA_TWO) * summed[layer].astype(jnp.float32)
@@ -1534,30 +1600,9 @@
     rates = jnp.where(row < bias_rows, RATE_BIAS, RATE_GAIN)
     vectors_new[...] = vectors[...] - rates * (vec[2] + DECAY * vectors[...])
 
-    for layer in range(layers):
-        for which in range(3):
-            load(which, layer).wait()
-        high, rest = halves(bases[layer])
-
-        def one_piece(index, carry):
-            here = pl.ds(pl.multiple_of(index * piece, piece), piece)
-            given = grads[layer, here, :]
-            rotated = mix(given, high, 1, 0) + mix(given, rest, 1, 0)
-            first_new, second_new, direction = moments(
-                rotated, first[layer, here, :], second[layer, here, :]
-            )
-            first[layer, here, :] = first_new
-            second[layer, here, :] = second_new
-            up, down = halves(direction)
-            back = mix(up, high, 1, 1) + (mix(up, rest, 1, 1) + mix(down, high, 1, 1))
-            old = master[layer, here, :]
-            master[layer, here, :] = old - RATE_CONV * (back + DECAY * old)
-            return carry
-
-        lax.fori_loop(0, rows // piece, one_piece, 0)
-        for which in range(3):
-            store(which, layer).start()
-
+    for which in range(moved):
+        take(which).wait()
+        give(which).start()
     eye = (
         lax.broadcasted_iota(jnp.int32, (block, block), 0)
         == lax.broadcasted_iota(jnp.int32, (block, block), 1)
@@ -1593,36 +1638,35 @@
     lax.fori_loop(0, channels // block, outer, 0)
     for layer in range(layers):
         bases_new[layer] = system[layer, :, channels : 2 * channels].T
-        for which in range(3):
-            store(which, layer).wait()
-
-
-def update(summed, statistics, bases, grads, conv, head, vector, bias_rows):
-    layers, rows, channels = grads.shape
-    piece = 144 if rows % 144 == 0 else rows
-    dims = (layers, rows, channels, piece, bias_rows, 32)
+    for which in range(moved):
+        give(which).wait()
+
+
+def update(arrays, summed, statistics, bases, head, vector, bias_rows):
+    layers, channels, unused = statistics.shape
+    dims = (layers, channels, bias_rows, 32, len(arrays))
+    anywhere = pl.BlockSpec(memory_space=pl.ANY)
     vmem = pl.BlockSpec(memory_space=pltpu.VMEM)
-    anywhere = pl.BlockSpec(memory_space=pl.ANY)
     square = jax.ShapeDtypeStruct(statistics.shape, jnp.float32)
-    tall = jax.ShapeDtypeStruct(grads.shape, jnp.float32)
     head_shape = jax.ShapeDtypeStruct(head[0].shape, jnp.float32)
     vector_shape = jax.ShapeDtypeStruct(vector[0].shape, jnp.float32)
     return pl.pallas_call(
         partial(update_kernel, dims),
-        out_shape=(square,) * 2 + (tall,) * 3 + (head_shape,) * 3 + (vector_shape,) * 3,
-        in_specs=[vmem] * 4 + [anywhere] * 3 + [vmem] * 8,
-        out_specs=[vmem] * 2 + [anywhere] * 3 + [vmem] * 6,
+        out_shape=tuple(jax.ShapeDtypeStruct(array.shape, array.dtype) for array in arrays)
+        + (square,) * 2 + (head_shape,) * 3 + (vector_shape,) * 3,
+        in_specs=[anywhere] * len(arrays) + [vmem] * 11,
+        out_specs=[anywhere] * len(arrays) + [vmem] * 8,
         scratch_shapes=[
             pltpu.VMEM((layers, channels, 2 * channels), jnp.float32),
             pltpu.VMEM((layers, LANES, 2 * channels), jnp.float32),
-            pltpu.VMEM(grads.shape, jnp.float32),
-            pltpu.VMEM(grads.shape, jnp.float32),
-            pltpu.VMEM(grads.shape, jnp.float32),
-            pltpu.SemaphoreType.DMA((3, layers)),
-            pltpu.SemaphoreType.DMA((3, layers)),
-        ],
+        ]
+        + [pltpu.VMEM(array.shape, array.dtype) for array in arrays]
+        + [pltpu.SemaphoreType.DMA((2, len(arrays)))],
         compiler_params=pltpu.CompilerParams(vmem_limit_bytes=VMEM_LIMIT),
-    )(summed, statistics, bases, grads, *conv, *head, *vector)
+        cost_estimate=pl.CostEstimate(
+            flops=10**10, bytes_accessed=2 * 10**7, transcendentals=10**4
+        ),
+    )(*arrays, summed, statistics, bases, *head, *vector)
 
 
 def local(
@@ -1662,23 +1706,26 @@
         valid_rows,
         space_count,
     )
-    owned_conv, summed_stats, grad_vec = reduce_grads(grads, vector, space_count)
+    summed_stats, grad_vec, conv_new = reduce_grads(
+        grads, vector, bases, (conv_first, conv_second, conv_master), space_count
+    )
+    moved = (merged, features_grad, *conv_new)
     outs = update(
+        moved,
         summed_stats,
         statistics,
         bases,
-        owned_conv,
-        (conv_first, conv_second, conv_master),
         (owned_head, head_first, head_second, head_master),
         (grad_vec, vec_first, vec_second, vectors),
         (3 * channels + head_width) // LANES,
     )
-    stats_new, bases_new = outs[:2]
+    merged, features_grad, *conv_new = outs[:5]
+    stats_new, bases_new = outs[5:7]
     return (
         merged.reshape(cotangent.shape),
         features_grad.reshape(features.shape),
-        *outs[2:5],
-        *(out.reshape(-1) for out in outs[5:]),
+        *conv_new,
+        *(out.reshape(-1) for out in outs[7:]),
         stats_new,
         bases_new,
     )

time: 331 us -> 314 us (0.949)
  Pallas kernels: 327 us -> 313 us
    pallas_call x1, Pallas kernels: 61.6 us -> 48.1 us  [update(): pl.pallas_call(partial(update_kernel, dims), out_shape=tuple((jax.ShapeDt...]
where the time goes in v1:
time: 314 us
  Pallas kernels  313 us (100%)
    pallas_call x1, Pallas kernels, reduce_grads(): pl.pallas_call(partial(reduce_kernel, layers, deep_count), out_shape=(jax...  114 us
    pallas_call x1, Pallas kernels, gather_weights(): pl.pallas_call(partial(gather_kernel, dims), out_shape=(jax.ShapeDtypeStr...  96.7 us
    pallas_call x1, Pallas kernels, run_block(): pl.pallas_call(partial(work_kernel, dims), out_shape=(jax.ShapeDtypeStruc...  54.8 us
    pallas_call x1, Pallas kernels, update(): pl.pallas_call(partial(update_kernel, dims), out_shape=tuple((jax.ShapeDt...  48.1 us

profile of v1, /device:TPU:0, one launch (start us, length us, event | category | flops | bytes accessed | tf_op | source)
XLA Modules:
  0.0 314.0 jit_solution(16645159343726261957)
XLA Ops:
  0.6 96.7 %shard_map.237 = (bf16[3,4,2,576,512]{4,3,2,1,0:T(8,128)(2,1)}, bf16[2,2,4,2,16,1792]{5,4,3,2,1,0:T(8,128)(2,1)}, bf16[3,768,1536]{2,1,0:T(8,128)(2,1)}, f32[3,512,512]{2,1,0:T(8,128)}, bf16[512,512]{1,0:T(8,128)(2,1)}) custom-call(f32[3,576,512]{2,1,0:T(8,128)} %master_in.1, f32[224,128]{1,0:T(8,128)} %bitcast.25, bf16[512,512]{1,0:T(8,128)(2,1)} %bitcast.24, ...), custom_call_target="tpu_custom_call" | custom-call | tf_op jit(solution)/shard_map/pallas_call | solution.py:537
  97.4 54.8 %shard_map.238 = (bf16[512,1792]{1,0:T(8,128)(2,1)}, bf16[512,512]{1,0:T(8,128)(2,1)}, bf16[3,4608,512]{2,1,0:T(8,128)(2,1)}, f32[224,128]{1,0:T(8,128)}, f32[40,128]{1,0:T(8,128)}) custom-call(bf16[3,4608,512]{2,1,0:T(8,128)(2,1)} %bitcast.21, bf16[512,1792]{1,0:T(8,128)(2,1)} %bitcast.23, bf16[3,768,1536]{2,1,0:T(8,128)(2,1)} %get-tuple-element.43.wide_in, ...), custom_call_target="tpu_custom_call" | custom-call | tf_op jit(solution)/shard_map/pallas_call | solution.py:1392
  152.2 113.5 %shard_map.239 = (bf16[3,576,512]{2,1,0:T(8,128)(2,1)}, bf16[3,4,128,512]{3,2,1,0:T(8,128)(2,1)}, f32[40,128]{1,0:T(8,128)}, f32[3,576,512]{2,1,0:T(8,128)}, f32...) custom-call(bf16[3,4,2,576,512]{4,3,2,1,0:T(8,128)(2,1)} %bitcast.20, f32[40,128]{1,0:T(8,128)} %get-tuple-element.49.vector, ...), custom_call_target="tpu_custom_call" | custom-call | tf_op jit(solution)/shard_map/pallas_call | solution.py:1013
  265.7 48.1 %shard_map.240 = (bf16[512,1792]{1,0:T(8,128)(2,1)}, bf16[512,512]{1,0:T(8,128)(2,1)}, f32[3,576,512]{2,1,0:T(8,128)}, f32[3,576,512]{2,1,0:T(8,128)}, f32[3,576...) custom-call(bf16[512,1792]{1,0:T(8,128)(2,1)} %get-tuple-element.46., ...), custom_call_target="tpu_custom_call" | custom-call | flops 10000000000 | bytes 20000000 | tf_op jit(solution)/shard_map/pallas_call | solution.py:1653

commit v2 on v1

--- a/solution.py
+++ b/solution.py
@@ -248,26 +248,39 @@
 
     chunks = layers * deep_count
 
+    def by_distance(index):
+        left, right = deep, deep_count - 1 - deep
+        short = jnp.minimum(left, right)
+        both = (index + 1) // 2 * (2 * lax.rem(index, 2) - 1)
+        one = (index - short) * jnp.where(left < right, 1, -1)
+        return deep + jnp.where(index <= 2 * short, both, one)
+
     def split(chunk):
         rest = chunk - layers
         is_own = chunk < layers
         layer = jnp.where(is_own, chunk, rest // (deep_count - 1))
         hop = jnp.where(is_own, 0, 1 + lax.rem(rest + chunks, deep_count - 1))
         layer, hop = jnp.clip(layer, 0, layers - 1), jnp.clip(hop, 0, deep_count - 1)
-        source = lax.rem(deep - hop + deep_count, deep_count)
-        return (layer, hop, source, lax.rem(chunk, 2))
-
-    def first(layer, hop):
+        source = by_distance(hop)
+        odd = jnp.where(is_own, 0, lax.rem(chunk, 2))
+        return (layer, hop, source, odd)
+
+    def first(layer, index):
         piece = own.at[layer, :, lanes(block)]
         target = full.at[layer, deep, side, :, lanes(block)]
-        to = at(across, core, lax.rem(deep + hop, deep_count), side)
-        return remote(piece, target, sends.at[0, layer, hop], receives.at[0, layer, hop], to)
-
-    def first_in(layer, hop):
-        source = lax.rem(deep - hop + deep_count, deep_count)
+        there = by_distance(index)
+        to = at(across, core, there, side)
+        return remote(piece, target, sends.at[0, layer, there], receives.at[0, layer, deep], to)
+
+    def first_in(layer, index):
+        source = by_distance(index)
         piece = full.at[layer, source, side, :, lanes(block)]
         return remote(
-            piece, piece, sends.at[0, layer, hop], receives.at[0, layer, hop], at(across, core, deep, side)
+            piece,
+            piece,
+            sends.at[0, layer, source],
+            receives.at[0, layer, source],
+            at(across, core, source, side),
         )
 
     def second(chunk, incoming):
@@ -302,11 +315,15 @@
         to = at(across, 1 - core, deep, side)
         return remote(piece, piece, sends.at[4, layer, hop], receives.at[4, layer, hop], to)
 
+    def own_fourth(layer, incoming):
+        column = 1 - core if incoming else core
+        piece = full.at[layer, deep, 1 - side, :, lanes(2 * column, 2)]
+        to = at(across, 1 - core, deep, side)
+        return remote(piece, piece, sends.at[4, layer, 0], receives.at[4, layer, 0], to)
+
     def local(layer):
         return pltpu.make_async_copy(
-            own.at[layer, :, lanes(block)],
-            full.at[layer, deep, side, :, lanes(block)],
-            local_sem.at[layer],
+            own.at[layer], full.at[layer, deep, side], local_sem.at[layer]
         )
 
     def each(low, action):
@@ -380,7 +397,7 @@
         )
 
     def arrive(layer):
-        fourth(layer, True).wait_recv()
+        own_fourth(layer, True).wait_recv()
         begin = layers + layer * (deep_count - 1)
         loop(deep_count - 1, lambda index: fourth(begin + index, True).wait_recv())
         loop(space_count, lambda owner: load(layer, owner).start())
@@ -433,26 +450,45 @@
         @pl.when(hop > 0)
         def other_rows():
             first_in(layer, hop).wait_recv()
+            go_first(chunk - layers + z_ahead)
 
         second(chunk, False).start()
 
     def go_third(chunk):
         second(chunk, True).wait_recv()
-        third(chunk, 0, False).start()
-        third(chunk, 1, False).start()
+
+        @pl.when(chunk < layers)
+        def own_rows():
+            third(chunk, 1 - side, False).start()
+
+        @pl.when(chunk >= layers)
+        def other_rows():
+            third(chunk, 0, False).start()
+            third(chunk, 1, False).start()
 
     def go_fourth(chunk):
-        third(chunk, 0, True).wait_recv()
-        third(chunk, 1, True).wait_recv()
-        fourth(chunk, False).start()
+        @pl.when(chunk < layers)
+        def own_rows():
+            third(chunk, 1 - side, True).wait_recv()
+            own_fourth(chunk, False).start()
+
+        @pl.when(chunk >= layers)
+        def other_rows():
+            third(chunk, 0, True).wait_recv()
+            third(chunk, 1, True).wait_recv()
+            fourth(chunk, False).start()
 
     def go_head_first():
         each(1, lambda hop: head_first(hop).start())
 
-    def go_first(layer):
-        each(1, lambda hop: first(layer, hop).start())
-
-    go_first(0)
+    def go_first(index):
+        @pl.when(index < layers * (deep_count - 1))
+        def more():
+            first(index // (deep_count - 1), 1 + lax.rem(index, deep_count - 1)).start()
+
+    z_ahead = 2
+    for index in range(min(z_ahead, deep_count - 1)):
+        go_first(index)
     local(0).start()
     go_second(0)
     for layer in range(1, layers):
@@ -470,15 +506,14 @@
             put(wide.at[0], row + 1, part * tile, tile, value.astype(jnp.float32))
     send_edges(0, wide.at[0])
 
-    lag_third, lag_fourth = 2, 5
+    lag_third, lag_fourth = 2, 4
     others = deep_count - 1
 
     def last_of(layer):
         return layers + others * (layer + 1) - 1 + lag_fourth
 
     early = min(2, others)
-    timed = [(layers + others * (layer - 1) + early, go_first, layer) for layer in range(1, layers)]
-    timed += [(layers + early, go_head_first)]
+    timed = [(layers + early, go_head_first)]
     timed += [(layers + others + 2 * which, go_head, which) for which in range(3)]
     for layer in range(layers - 1):
         timed += [(last_of(layer) + 1, arrive, layer), (last_of(layer) + 2, forward, layer)]
@@ -505,9 +540,17 @@
 
     def finish(chunk):
         second(chunk, False).wait_send()
-        third(chunk, 0, False).wait_send()
-        third(chunk, 1, False).wait_send()
-        fourth(chunk, False).wait_send()
+
+        @pl.when(chunk < layers)
+        def own_rows():
+            third(chunk, 1 - side, False).wait_send()
+            own_fourth(chunk, False).wait_send()
+
+        @pl.when(chunk >= layers)
+        def other_rows():
+            third(chunk, 0, False).wait_send()
+            third(chunk, 1, False).wait_send()
+            fourth(chunk, False).wait_send()
 
     loop(chunks, finish)
     each(1, lambda hop: head_first(hop).wait_send())
@@ -938,16 +981,16 @@
             vector_deep[deep] = summed
             run(1, deep_count, lambda hop: vector_along(hop).start())
 
-    chunk_work = ((0, go_second), (2, go_third), (4, go_fourth))
+    chunk_work = ((0, go_second), (2, go_third), (3, go_fourth))
     layer_work = (
-        (6, close),
-        (7, spread),
-        (8, measure),
-        (9, pair),
-        (10, refresh),
-        (11, settle),
-        (12, share_core),
-        (13, finish),
+        (4, close),
+        (5, spread),
+        (6, measure),
+        (7, pair),
+        (8, refresh),
+        (9, settle),
+        (10, share_core),
+        (11, finish),
     )
     vector_out[0] = vector[...]
     vector_step(0).start()

time: 314 us -> 307 us (0.978)
  Pallas kernels: 313 us -> 305 us
    pallas_call x1, Pallas kernels: 114 us -> 108 us  [reduce_grads(): pl.pallas_call(partial(reduce_kernel, layers, deep_count), out_shape=(jax...]
where the time goes in v2:
time: 307 us; the launch traced here: 306 us
  Pallas kernels  305 us (99%)
    pallas_call x1, Pallas kernels, reduce_grads(): pl.pallas_call(partial(reduce_kernel, layers, deep_count), out_shape=(jax...  108 us
    pallas_call x1, Pallas kernels, gather_weights(): pl.pallas_call(partial(gather_kernel, dims), out_shape=(jax.ShapeDtypeStr...  96.4 us
    pallas_call x1, Pallas kernels, run_block(): pl.pallas_call(partial(work_kernel, dims), out_shape=(jax.ShapeDtypeStruc...  53.1 us
    pallas_call x1, Pallas kernels, update(): pl.pallas_call(partial(update_kernel, dims), out_shape=tuple((jax.ShapeDt...  48.1 us

profile of v2, /device:TPU:0, one launch (start us, length us, event | category | flops | bytes accessed | tf_op | source)
XLA Modules:
  0.0 306.1 jit_solution(18264843349870575422)
XLA Ops:
  0.6 96.4 %shard_map.237 = (bf16[3,4,2,576,512]{4,3,2,1,0:T(8,128)(2,1)}, bf16[2,2,4,2,16,1792]{5,4,3,2,1,0:T(8,128)(2,1)}, bf16[3,768,1536]{2,1,0:T(8,128)(2,1)}, f32[3,512,512]{2,1,0:T(8,128)}, bf16[512,512]{1,0:T(8,128)(2,1)}) custom-call(f32[3,576,512]{2,1,0:T(8,128)} %master_in.1, f32[224,128]{1,0:T(8,128)} %bitcast.25, bf16[512,512]{1,0:T(8,128)(2,1)} %bitcast.24, ...), custom_call_target="tpu_custom_call" | custom-call | tf_op jit(solution)/shard_map/pallas_call | solution.py:580
  97.0 53.1 %shard_map.238 = (bf16[512,1792]{1,0:T(8,128)(2,1)}, bf16[512,512]{1,0:T(8,128)(2,1)}, bf16[3,4608,512]{2,1,0:T(8,128)(2,1)}, f32[224,128]{1,0:T(8,128)}, f32[40,128]{1,0:T(8,128)}) custom-call(bf16[3,4608,512]{2,1,0:T(8,128)(2,1)} %bitcast.21, bf16[512,1792]{1,0:T(8,128)(2,1)} %bitcast.23, bf16[3,768,1536]{2,1,0:T(8,128)(2,1)} %get-tuple-element.43.wide_in, ...), custom_call_target="tpu_custom_call" | custom-call | tf_op jit(solution)/shard_map/pallas_call | solution.py:1435
  150.2 107.7 %shard_map.239 = (bf16[3,576,512]{2,1,0:T(8,128)(2,1)}, bf16[3,4,128,512]{3,2,1,0:T(8,128)(2,1)}, f32[40,128]{1,0:T(8,128)}, f32[3,576,512]{2,1,0:T(8,128)}, f32...) custom-call(bf16[3,4,2,576,512]{4,3,2,1,0:T(8,128)(2,1)} %bitcast.20, f32[40,128]{1,0:T(8,128)} %get-tuple-element.49.vector, ...), custom_call_target="tpu_custom_call" | custom-call | tf_op jit(solution)/shard_map/pallas_call | solution.py:1056
  257.9 48.1 %shard_map.240 = (bf16[512,1792]{1,0:T(8,128)(2,1)}, bf16[512,512]{1,0:T(8,128)(2,1)}, f32[3,576,512]{2,1,0:T(8,128)}, f32[3,576,512]{2,1,0:T(8,128)}, f32[3,576...) custom-call(bf16[512,1792]{1,0:T(8,128)(2,1)} %get-tuple-element.46., ...), custom_call_target="tpu_custom_call" | custom-call | flops 10000000000 | bytes 20000000 | tf_op jit(solution)/shard_map/pallas_call | solution.py:1696

commit v3 on v2

--- a/solution.py
+++ b/solution.py
@@ -1379,6 +1379,8 @@
         loop(TAPS * TAPS, one_tap)
         store(layer).start()
         head_next(layers - 1 - layer)
+        if layer == 0:
+            loop(heads, term_total)
         take_edges(which, d_wide)
 
         def back(part):
@@ -1397,7 +1399,6 @@
 
         loop(tiles, back)
 
-    loop(heads, term_total)
     features_grad[...] = d_active[...].astype(low)
     head_end()
     loop(heads, term_end)
@@ -1611,7 +1612,8 @@
     vector_second_new,
     vectors_new,
     system,
-    pivot,
+    pivot_high,
+    pivot_rest,
 ):
     layers, channels, bias_rows, panel, moved = dims
     block = LANES
@@ -1664,15 +1666,49 @@
                     panels[layer] = panels[layer][panel:] - dot(
                         tops[layer][:, panel * (j + 1) : block], tops[layer], 0, 0
                     )
-        for layer in range(layers):
-            inverse = jnp.concatenate(done[layer], 0)
-            pivot[layer] = dot(inverse, system[layer, here, :], 1, 0)
-            system[layer, here, channels : 2 * channels] = pivot[layer, :, channels : 2 * channels]
+        half = channels // 2
+        spans = (slice(0, half), slice(half, channels), slice(channels, 2 * channels))
+        after = (k + 1) * block
+        split_inverse = [halves(jnp.concatenate(parts, 0)) for parts in done]
+
+        def eliminated(span):
+            for layer in range(layers):
+                high, rest = split_inverse[layer]
+                right_high, right_rest = halves(system[layer, here, span])
+                value = mix(high, right_high, 1, 0) + (
+                    mix(high, right_rest, 1, 0) + mix(rest, right_high, 1, 0)
+                )
+                pivot_high[layer, :, span], pivot_rest[layer, :, span] = halves(value)
+                if span is spans[2]:
+                    system[layer, here, span] = value
+
+        eliminated(spans[2])
+
+        @pl.when(after < channels)
+        def right_half():
+            eliminated(spans[1])
+
+        @pl.when(after < half)
+        def left_half():
+            eliminated(spans[0])
 
         def inner(i, carry_in):
             below = pl.ds(pl.multiple_of(i * block, block), block)
-            for layer in range(layers):
-                system[layer, below, :] -= dot(pivot[layer, :, below], pivot[layer], 0, 0)
+
+            def subtract(span):
+                for layer in range(layers):
+                    left_high, left_rest = pivot_high[layer, :, below], pivot_rest[layer, :, below]
+                    right_high, right_rest = pivot_high[layer, :, span], pivot_rest[layer, :, span]
+                    system[layer, below, span] -= mix(left_high, right_high, 0, 0) + (
+                        mix(left_high, right_rest, 0, 0) + mix(left_rest, right_high, 0, 0)
+                    )
+
+            subtract(slice(half, 2 * channels))
+
+            @pl.when(i * block < half)
+            def left_half():
+                subtract(spans[0])
+
             return carry_in
 
         lax.fori_loop(k + 1, channels // block, inner, 0)
@@ -1701,7 +1737,8 @@
         out_specs=[anywhere] * len(arrays) + [vmem] * 8,
         scratch_shapes=[
             pltpu.VMEM((layers, channels, 2 * channels), jnp.float32),
-            pltpu.VMEM((layers, LANES, 2 * channels), jnp.float32),
+            pltpu.VMEM((layers, LANES, 2 * channels), jnp.bfloat16),
+            pltpu.VMEM((layers, LANES, 2 * channels), jnp.bfloat16),
         ]
         + [pltpu.VMEM(array.shape, array.dtype) for array in arrays]
         + [pltpu.SemaphoreType.DMA((2, len(arrays)))],

time: 307 us -> 305 us (level)
  no operation moved by 1% of the time
where the time goes in v3:
time: 305 us
  Pallas kernels  304 us (100%)
    pallas_call x1, Pallas kernels, reduce_grads(): pl.pallas_call(partial(reduce_kernel, layers, deep_count), out_shape=(jax...  108 us
    pallas_call x1, Pallas kernels, gather_weights(): pl.pallas_call(partial(gather_kernel, dims), out_shape=(jax.ShapeDtypeStr...  96.4 us
    pallas_call x1, Pallas kernels, run_block(): pl.pallas_call(partial(work_kernel, dims), out_shape=(jax.ShapeDtypeStruc...  52.5 us
    pallas_call x1, Pallas kernels, update(): pl.pallas_call(partial(update_kernel, dims), out_shape=tuple((jax.ShapeDt...  46.5 us

profile of v3, /device:TPU:0, one launch (start us, length us, event | category | flops | bytes accessed | tf_op | source)
XLA Modules:
  0.0 304.6 jit_solution(8893655855080379385)
XLA Ops:
  0.6 96.4 %shard_map.237 = (bf16[3,4,2,576,512]{4,3,2,1,0:T(8,128)(2,1)}, bf16[2,2,4,2,16,1792]{5,4,3,2,1,0:T(8,128)(2,1)}, bf16[3,768,1536]{2,1,0:T(8,128)(2,1)}, f32[3,512,512]{2,1,0:T(8,128)}, bf16[512,512]{1,0:T(8,128)(2,1)}) custom-call(f32[3,576,512]{2,1,0:T(8,128)} %master_in.1, f32[224,128]{1,0:T(8,128)} %bitcast.25, bf16[512,512]{1,0:T(8,128)(2,1)} %bitcast.24, ...), custom_call_target="tpu_custom_call" | custom-call | tf_op jit(solution)/shard_map/pallas_call | solution.py:580
  97.0 52.5 %shard_map.238 = (bf16[512,1792]{1,0:T(8,128)(2,1)}, bf16[512,512]{1,0:T(8,128)(2,1)}, bf16[3,4608,512]{2,1,0:T(8,128)(2,1)}, f32[224,128]{1,0:T(8,128)}, f32[40,128]{1,0:T(8,128)}) custom-call(bf16[3,4608,512]{2,1,0:T(8,128)(2,1)} %bitcast.21, bf16[512,1792]{1,0:T(8,128)(2,1)} %bitcast.23, bf16[3,768,1536]{2,1,0:T(8,128)(2,1)} %get-tuple-element.43.wide_in, ...), custom_call_target="tpu_custom_call" | custom-call | tf_op jit(solution)/shard_map/pallas_call | solution.py:1436
  149.5 108.4 %shard_map.239 = (bf16[3,576,512]{2,1,0:T(8,128)(2,1)}, bf16[3,4,128,512]{3,2,1,0:T(8,128)(2,1)}, f32[40,128]{1,0:T(8,128)}, f32[3,576,512]{2,1,0:T(8,128)}, f32...) custom-call(bf16[3,4,2,576,512]{4,3,2,1,0:T(8,128)(2,1)} %bitcast.20, f32[40,128]{1,0:T(8,128)} %get-tuple-element.49.vector, ...), custom_call_target="tpu_custom_call" | custom-call | tf_op jit(solution)/shard_map/pallas_call | solution.py:1056
  257.9 46.5 %shard_map.240 = (bf16[512,1792]{1,0:T(8,128)(2,1)}, bf16[512,512]{1,0:T(8,128)(2,1)}, f32[3,576,512]{2,1,0:T(8,128)}, f32[3,576,512]{2,1,0:T(8,128)}, f32[3,576...) custom-call(bf16[512,1792]{1,0:T(8,128)(2,1)} %get-tuple-element.46., ...), custom_call_target="tpu_custom_call" | custom-call | flops 10000000000 | bytes 20000000 | tf_op jit(solution)/shard_map/pallas_call | solution.py:1732

commit v4 on v3

--- a/solution.py
+++ b/solution.py
@@ -60,6 +60,14 @@
 
 def lanes(index, count=1):
     return pl.ds(pl.multiple_of(index * LANES, LANES), count * LANES)
+
+
+def nearest(deep, deep_count, index):
+    left, right = deep, deep_count - 1 - deep
+    short = jnp.minimum(left, right)
+    both = (index + 1) // 2 * (2 * lax.rem(index, 2) - 1)
+    one = (index - short) * jnp.where(left < right, 1, -1)
+    return deep + jnp.where(index <= 2 * short, both, one)
 
 
 def partners(deep_count):
@@ -249,11 +257,7 @@
     chunks = layers * deep_count
 
     def by_distance(index):
-        left, right = deep, deep_count - 1 - deep
-        short = jnp.minimum(left, right)
-        both = (index + 1) // 2 * (2 * lax.rem(index, 2) - 1)
-        one = (index - short) * jnp.where(left < right, 1, -1)
-        return deep + jnp.where(index <= 2 * short, both, one)
+        return nearest(deep, deep_count, index)
 
     def split(chunk):
         rest = chunk - layers
@@ -668,9 +672,8 @@
     steps = layers * deep_count
 
     def split(step):
-        layer, hop = step // deep_count, lax.rem(step + 1, deep_count)
-        target = lax.rem(deep + hop, deep_count)
-        return (layer, hop, target, lax.rem(target, 2))
+        layer, hop = step // deep_count, deep_count - 1 - lax.rem(step, deep_count)
+        return (layer, hop, nearest(deep, deep_count, hop), lax.rem(step, 2))
 
     def first(step):
         layer, hop, target, odd = split(step)
@@ -715,12 +718,27 @@
 
     def fourth(step):
         layer, hop, target, odd = split(step)
+        slot = layer * deep_count + deep
         return remote(
             last.at[step],
-            last_in.at[step],
+            last_in.at[slot],
             sends.at[4, step],
-            receives.at[4, step],
+            receives.at[4, slot],
             at(across, core, target, side),
+        )
+
+    def fourth_in(layer, hop):
+        source = nearest(deep, deep_count, hop)
+        slot = layer * deep_count + source
+        return (
+            slot,
+            remote(
+                last_in.at[slot],
+                last_in.at[slot],
+                sends.at[4, slot],
+                receives.at[4, slot],
+                at(across, core, source, side),
+            ),
         )
 
     def fifth(layer, incoming):
@@ -893,9 +911,9 @@
         acc[...] = last[layer * deep_count + deep_count - 1].astype(jnp.float32)
 
         def add(hop):
-            step = layer * deep_count + hop - 1
-            fourth(step).wait_recv()
-            acc[...] += last_in[step].astype(jnp.float32)
+            slot, copy = fourth_in(layer, hop)
+            copy.wait_recv()
+            acc[...] += last_in[slot].astype(jnp.float32)
 
         run(1, deep_count, add)
         total[layer, :, lanes(block)] = acc[...].astype(jnp.bfloat16)

time: 305 us -> 302 us (level)
  no operation moved by 1% of the time
where the time goes in v4:
time: 302 us
  Pallas kernels  301 us (100%)
    pallas_call x1, Pallas kernels, reduce_grads(): pl.pallas_call(partial(reduce_kernel, layers, deep_count), out_shape=(jax...  106 us
    pallas_call x1, Pallas kernels, gather_weights(): pl.pallas_call(partial(gather_kernel, dims), out_shape=(jax.ShapeDtypeStr...  96.4 us
    pallas_call x1, Pallas kernels, run_block(): pl.pallas_call(partial(work_kernel, dims), out_shape=(jax.ShapeDtypeStruc...  52.5 us
    pallas_call x1, Pallas kernels, update(): pl.pallas_call(partial(update_kernel, dims), out_shape=tuple((jax.ShapeDt...  46.5 us

profile of v4, /device:TPU:0, one launch (start us, length us, event | category | flops | bytes accessed | tf_op | source)
XLA Modules:
  0.0 302.2 jit_solution(5201973750259314434)
XLA Ops:
  0.6 96.4 %shard_map.237 = (bf16[3,4,2,576,512]{4,3,2,1,0:T(8,128)(2,1)}, bf16[2,2,4,2,16,1792]{5,4,3,2,1,0:T(8,128)(2,1)}, bf16[3,768,1536]{2,1,0:T(8,128)(2,1)}, f32[3,512,512]{2,1,0:T(8,128)}, bf16[512,512]{1,0:T(8,128)(2,1)}) custom-call(f32[3,576,512]{2,1,0:T(8,128)} %master_in.1, f32[224,128]{1,0:T(8,128)} %bitcast.25, bf16[512,512]{1,0:T(8,128)(2,1)} %bitcast.24, ...), custom_call_target="tpu_custom_call" | custom-call | tf_op jit(solution)/shard_map/pallas_call | solution.py:584
  97.0 52.5 %shard_map.238 = (bf16[512,1792]{1,0:T(8,128)(2,1)}, bf16[512,512]{1,0:T(8,128)(2,1)}, bf16[3,4608,512]{2,1,0:T(8,128)(2,1)}, f32[224,128]{1,0:T(8,128)}, f32[40,128]{1,0:T(8,128)}) custom-call(bf16[3,4608,512]{2,1,0:T(8,128)(2,1)} %bitcast.21, bf16[512,1792]{1,0:T(8,128)(2,1)} %bitcast.23, bf16[3,768,1536]{2,1,0:T(8,128)(2,1)} %get-tuple-element.43.wide_in, ...), custom_call_target="tpu_custom_call" | custom-call | tf_op jit(solution)/shard_map/pallas_call | solution.py:1454
  149.5 106.0 %shard_map.239 = (bf16[3,576,512]{2,1,0:T(8,128)(2,1)}, bf16[3,4,128,512]{3,2,1,0:T(8,128)(2,1)}, f32[40,128]{1,0:T(8,128)}, f32[3,576,512]{2,1,0:T(8,128)}, f32...) custom-call(bf16[3,4,2,576,512]{4,3,2,1,0:T(8,128)(2,1)} %bitcast.20, f32[40,128]{1,0:T(8,128)} %get-tuple-element.49.vector, ...), custom_call_target="tpu_custom_call" | custom-call | tf_op jit(solution)/shard_map/pallas_call | solution.py:1074
  255.5 46.5 %shard_map.240 = (bf16[512,1792]{1,0:T(8,128)(2,1)}, bf16[512,512]{1,0:T(8,128)(2,1)}, f32[3,576,512]{2,1,0:T(8,128)}, f32[3,576,512]{2,1,0:T(8,128)}, f32[3,576...) custom-call(bf16[512,1792]{1,0:T(8,128)(2,1)} %get-tuple-element.46., ...), custom_call_target="tpu_custom_call" | custom-call | flops 10000000000 | bytes 20000000 | tf_op jit(solution)/shard_map/pallas_call | solution.py:1750

commit v5 on v4

--- a/solution.py
+++ b/solution.py
@@ -219,7 +219,7 @@
 
 def gather_kernel(
     dims,
-    master,
+    master_in,
     head_master,
     features,
     vectors,
@@ -245,12 +245,23 @@
     store_sem,
     edge_sends,
     edge_receives,
+    master,
+    master_sem,
 ):
     layers, rows, width, channels, heads, depth, space_count = dims
     deep_count = space_count // 2
     across, core, deep, side = place()
     block = 2 * core + across
     low = jnp.bfloat16
+
+    def fetch(layer):
+        return pltpu.make_async_copy(
+            master_in.at[layer], master.at[layer], master_sem.at[layer]
+        )
+
+    for layer in range(layers):
+        fetch(layer).start()
+    fetch(0).wait()
     own[0] = master[0].astype(low)
     greet_edges(partners(deep_count), space_count)
 
@@ -496,6 +507,7 @@
     local(0).start()
     go_second(0)
     for layer in range(1, layers):
+        fetch(layer).wait()
         own[layer] = master[layer].astype(low)
         local(layer).start()
     head_rows, head_blocks = head_own.shape[0], heads * depth // LANES
@@ -590,7 +602,7 @@
             jax.ShapeDtypeStruct((layers, pixels, channels), wide_float),
             jax.ShapeDtypeStruct((pixels, channels), low),
         ),
-        in_specs=[vmem] * 4 + [pl.BlockSpec(memory_space=pltpu.SMEM)],
+        in_specs=[anywhere] + [vmem] * 3 + [pl.BlockSpec(memory_space=pltpu.SMEM)],
         out_specs=[anywhere] * 5,
         scratch_shapes=[
             pltpu.VMEM(master.shape, low),
@@ -609,6 +621,8 @@
             pltpu.SemaphoreType.DMA((3, layers)),
             pltpu.SemaphoreType.DMA((layers, 2)),
             pltpu.SemaphoreType.DMA((layers, 2)),
+            pltpu.VMEM(master.shape, wide_float),
+            pltpu.SemaphoreType.DMA((layers,)),
         ],
         compiler_params=pltpu.CompilerParams(
             collective_id=0, has_side_effects=True, vmem_limit_bytes=VMEM_LIMIT

time: 302 us -> 303 us (level)
  no operation moved by 1% of the time
where the time goes in v5:
time: 303 us
  Pallas kernels  302 us (100%)
    pallas_call x1, Pallas kernels, reduce_grads(): pl.pallas_call(partial(reduce_kernel, layers, deep_count), out_shape=(jax...  107 us
    pallas_call x1, Pallas kernels, gather_weights(): pl.pallas_call(partial(gather_kernel, dims), out_shape=(jax.ShapeDtypeStr...  96.6 us
    pallas_call x1, Pallas kernels, run_block(): pl.pallas_call(partial(work_kernel, dims), out_shape=(jax.ShapeDtypeStruc...  52.5 us
    pallas_call x1, Pallas kernels, update(): pl.pallas_call(partial(update_kernel, dims), out_shape=tuple((jax.ShapeDt...  46.5 us

profile of v5, /device:TPU:0, one launch (start us, length us, event | category | flops | bytes accessed | tf_op | source)
XLA Modules:
  0.0 303.1 jit_solution(18325604807156806538)
XLA Ops:
  0.6 96.6 %shard_map.237 = (bf16[3,4,2,576,512]{4,3,2,1,0:T(8,128)(2,1)}, bf16[2,2,4,2,16,1792]{5,4,3,2,1,0:T(8,128)(2,1)}, bf16[3,768,1536]{2,1,0:T(8,128)(2,1)}, f32[3,512,512]{2,1,0:T(8,128)}, bf16[512,512]{1,0:T(8,128)(2,1)}) custom-call(f32[3,576,512]{2,1,0:T(8,128)} %master_in.3, f32[224,128]{1,0:T(8,128)} %bitcast.25, bf16[512,512]{1,0:T(8,128)(2,1)} %bitcast.24, ...), custom_call_target="tpu_custom_call" | custom-call | tf_op jit(solution)/shard_map/pallas_call | solution.py:596
  97.2 52.5 %shard_map.238 = (bf16[512,1792]{1,0:T(8,128)(2,1)}, bf16[512,512]{1,0:T(8,128)(2,1)}, bf16[3,4608,512]{2,1,0:T(8,128)(2,1)}, f32[224,128]{1,0:T(8,128)}, f32[40,128]{1,0:T(8,128)}) custom-call(bf16[3,4608,512]{2,1,0:T(8,128)(2,1)} %bitcast.21, bf16[512,1792]{1,0:T(8,128)(2,1)} %bitcast.23, bf16[3,768,1536]{2,1,0:T(8,128)(2,1)} %get-tuple-element.43.wide_in, ...), custom_call_target="tpu_custom_call" | custom-call | tf_op jit(solution)/shard_map/pallas_call | solution.py:1468
  149.7 106.7 %shard_map.239 = (bf16[3,576,512]{2,1,0:T(8,128)(2,1)}, bf16[3,4,128,512]{3,2,1,0:T(8,128)(2,1)}, f32[40,128]{1,0:T(8,128)}, f32[3,576,512]{2,1,0:T(8,128)}, f32...) custom-call(bf16[3,4,2,576,512]{4,3,2,1,0:T(8,128)(2,1)} %bitcast.20, f32[40,128]{1,0:T(8,128)} %get-tuple-element.49.vector, ...), custom_call_target="tpu_custom_call" | custom-call | tf_op jit(solution)/shard_map/pallas_call | solution.py:1088
  256.4 46.5 %shard_map.240 = (bf16[512,1792]{1,0:T(8,128)(2,1)}, bf16[512,512]{1,0:T(8,128)(2,1)}, f32[3,576,512]{2,1,0:T(8,128)}, f32[3,576,512]{2,1,0:T(8,128)}, f32[3,576...) custom-call(bf16[512,1792]{1,0:T(8,128)(2,1)} %get-tuple-element.46., ...), custom_call_target="tpu_custom_call" | custom-call | flops 10000000000 | bytes 20000000 | tf_op jit(solution)/shard_map/pallas_call | solution.py:1764
